TPU v7x, 256 devices: a whole 4x4x8 slice. The times are simulated.
256 devices in a mesh: blk: 32 (over z, x_lo, core), group: 8 (over y, x_hi).
Axes of the slice: x: 4 (x_hi: 2, x_lo: 2; x = x_hi * 2 + x_lo), y: 4, z: 8, core: 2. Of those that a mesh axis runs over, the one named last changes fastest.
Arguments:
- picture_pooled_states: bfloat16 [65536, 1536], P(('blk', 'group')), may hold values from -6 to 6
- caption_pooled_states: bfloat16 [65536, 1536], P(('blk', 'group')), may hold values from -6 to 6
- picture_rescale_factor: float32 [1536], replicated, may hold values from 0.1 to 1.9
- caption_rescale_factor: float32 [1536], replicated, may hold values from 0.1 to 1.9
- picture_head_matrix: bfloat16 [1536, 1024], replicated, may hold values from -0.15625 to 0.15625
- caption_head_matrix: bfloat16 [1536, 1024], replicated, may hold values from -0.15625 to 0.15625
- sharpness_factor: float32 [1], replicated, may hold values from 30 to 100
- score_offset_term: float32 [1], replicated, may hold values from -10 to -5
Outputs:
- image_feature_gradient: float32 [65536, 1536], P(('blk', 'group'))
- text_feature_gradient: float32 [65536, 1536], P(('blk', 'group'))
- img_weight_grad: float32 [1536, 1024], P('blk', 'group')
- txt_weight_grad: float32 [1536, 1024], P('blk', 'group')
All inputs are finite; a program needn't handle non-finite values.
Results may differ from a plain program's by a relative error of at most 0.025.
Values may be sent and summed in bfloat16 or wider, within the bound.
A program may use at most 128 MiB of HBM per device.

v0:
```python
import math

import jax
import jax.numpy as jnp
from jax import lax
from jax.sharding import PartitionSpec as P


def from_behind(shard, axis, by):
    size = lax.axis_size(axis)
    return lax.ppermute(shard, axis, [(i, (i + by) % size) for i in range(size)])


def projection_forward(feats, norm_gain, projection_weight):
    values = feats.astype(jnp.float32)
    feature_average = jnp.mean(values, axis=-1, keepdims=True)
    centered_input = values - feature_average
    inverse_deviation = lax.rsqrt(
        jnp.mean(centered_input * centered_input, axis=-1, keepdims=True) + 1e-06
    )
    normalized_input = centered_input * inverse_deviation
    activation = (normalized_input * norm_gain).astype(jnp.bfloat16)
    proj = jnp.dot(activation, projection_weight, preferred_element_type=jnp.float32)
    inverse_norm = lax.rsqrt(jnp.sum(proj * proj, axis=-1, keepdims=True) + 1e-06)
    unit_vector = proj * inverse_norm
    return (
        normalized_input,
        inverse_deviation,
        activation,
        unit_vector,
        inverse_norm,
        unit_vector.astype(jnp.bfloat16),
    )


def projection_backward(
    embedding_gradient,
    norm_gain,
    projection_weight,
    normalized_input,
    inverse_deviation,
    activation,
    unit_vector,
    inverse_norm,
):
    dproj = (
        (
            embedding_gradient
            - unit_vector * jnp.sum(unit_vector * embedding_gradient, axis=-1, keepdims=True)
        )
        * inverse_norm
    ).astype(jnp.bfloat16)
    d_act = jnp.dot(dproj, projection_weight.T, preferred_element_type=jnp.float32)
    normalized_gradient = d_act * norm_gain
    feature_gradient = inverse_deviation * (
        normalized_gradient
        - jnp.mean(normalized_gradient, axis=-1, keepdims=True)
        - normalized_input
        * jnp.mean(normalized_gradient * normalized_input, axis=-1, keepdims=True)
    )
    w_grad = jnp.dot(activation.T, dproj, preferred_element_type=jnp.float32)
    return (feature_gradient, w_grad)


def matched_tile(
    picture_latents,
    caption_latents,
    starting_position,
    sharpness_parameter,
    displacement_amount,
    matching_label,
):
    similarity_matrix = jnp.dot(
        picture_latents, caption_latents.T, preferred_element_type=jnp.float32
    )
    sigmoid_likelihood = jax.nn.sigmoid(
        sharpness_parameter * similarity_matrix + displacement_amount
    )
    if matching_label:
        row_ids = jnp.arange(picture_latents.shape[0], dtype=jnp.int32)[:, None] + starting_position
        col_ids = jnp.arange(caption_latents.shape[0], dtype=jnp.int32)[None, :]
        sigmoid_likelihood = sigmoid_likelihood - (row_ids == col_ids).astype(jnp.float32)
    pairwise_multiplier = sigmoid_likelihood.astype(jnp.bfloat16)
    picture_side_derivs = sharpness_parameter * jnp.dot(
        pairwise_multiplier, caption_latents, preferred_element_type=jnp.float32
    )
    caption_side_derivs = sharpness_parameter * jnp.dot(
        pairwise_multiplier.T, picture_latents, preferred_element_type=jnp.float32
    )
    return (picture_side_derivs, caption_side_derivs)


def on_device(
    picture_pooled_states,
    caption_pooled_states,
    picture_rescale_factor,
    caption_rescale_factor,
    picture_head_matrix,
    caption_head_matrix,
    sharpness_factor,
    score_offset_term,
):
    sharpness_parameter = sharpness_factor[0]
    displacement_amount = score_offset_term[0]
    rows = picture_pooled_states.shape[0]
    width = picture_head_matrix.shape[1]
    batch = rows * lax.axis_size("group") * lax.axis_size("blk")
    (
        image_normalized_input,
        image_inverse_std,
        image_activation,
        image_unit_vector,
        image_inverse_norm,
        picture_latent,
    ) = projection_forward(picture_pooled_states, picture_rescale_factor, picture_head_matrix)
    (
        text_normalized_input,
        text_inverse_std,
        text_activation,
        text_unit_vector,
        text_inverse_norm,
        text_embedding,
    ) = projection_forward(caption_pooled_states, caption_rescale_factor, caption_head_matrix)
    caption_cluster = lax.all_gather(text_embedding, "group", axis=0, tiled=True)
    starting_position = lax.axis_index("group") * rows
    local_picture_share, local_caption_share = matched_tile(
        picture_latent,
        caption_cluster,
        starting_position,
        sharpness_parameter,
        displacement_amount,
        True,
    )
    preceding_captions = from_behind(caption_cluster, "blk", 1)
    remote_picture_share, remote_caption_share = matched_tile(
        picture_latent, preceding_captions, 0, sharpness_parameter, displacement_amount, False
    )
    returned = from_behind(remote_caption_share.astype(jnp.bfloat16), "blk", -1).astype(
        remote_caption_share.dtype
    )
    image_embedding_gradient = local_picture_share + remote_picture_share
    d_txt_terms = local_caption_share + returned
    text_embedding_gradient = lax.psum_scatter(
        d_txt_terms.astype(jnp.bfloat16), "group", scatter_dimension=0, tiled=True
    ).astype(jnp.float32)
    image_feature_gradient, image_weight_gradient = projection_backward(
        image_embedding_gradient,
        picture_rescale_factor,
        picture_head_matrix,
        image_normalized_input,
        image_inverse_std,
        image_activation,
        image_unit_vector,
        image_inverse_norm,
    )
    text_feature_gradient, text_weight_gradient = projection_backward(
        text_embedding_gradient,
        caption_rescale_factor,
        caption_head_matrix,
        text_normalized_input,
        text_inverse_std,
        text_activation,
        text_unit_vector,
        text_inverse_norm,
    )
    inner_img, inner_txt = (
        lax.psum_scatter(
            image_weight_gradient.astype(jnp.bfloat16), "group", scatter_dimension=1, tiled=True
        ).astype(jnp.float32),
        lax.psum_scatter(
            text_weight_gradient.astype(jnp.bfloat16), "group", scatter_dimension=1, tiled=True
        ).astype(jnp.float32),
    )
    outer_img, outer_txt = (
        lax.psum_scatter(
            inner_img.astype(jnp.bfloat16), "blk", scatter_dimension=0, tiled=True
        ).astype(jnp.float32),
        lax.psum_scatter(
            inner_txt.astype(jnp.bfloat16), "blk", scatter_dimension=0, tiled=True
        ).astype(jnp.float32),
    )
    scale = math.sqrt(width / batch)
    return (image_feature_gradient, text_feature_gradient, outer_img * scale, outer_txt * scale)


def solution(mesh):
    in_specs = (P(("blk", "group"), None), P(("blk", "group"), None), P(), P(), P(), P(), P(), P())
    out_specs = (
        P(("blk", "group"), None),
        P(("blk", "group"), None),
        P("blk", "group"),
        P("blk", "group"),
    )
    return jax.shard_map(
        on_device, mesh=mesh, in_specs=in_specs, out_specs=out_specs, check_vma=False
    )
```

profile of v0, /device:TPU:1, one launch (start us, length us, event | category | flops | bytes accessed | tf_op | source)
XLA Modules:
  0.0 700.0 jit_solution(462055812117572445)
XLA Ops:
  7.2 0.0 copy-start
  7.2 0.0 copy-start.14
  7.2 0.0 all-gather.2.cloned.1.call-start
  7.2 0.0 copy-start.5
  7.2 1.5 convert_reduce_fusion
  8.7 1.5 fusion.27
  10.2 0.0 copy-done.14
  10.2 3.0 multiply_reduce_fusion.1
  13.3 1.1 copy-done.1
  14.4 0.9 multiply_convert_fusion.2
  15.3 0.0 all-gather.2.cloned.1.call-update
  15.3 0.0 reduce-scatter.16.cloned.1.call-start
  15.4 79.9 %all-gather.2.cloned.1.call-done = bf16[2048,1024]{1,0:T(8,128)(2,1)} async-done(((bf16[256,1024]{1,0:T(8,128)(2,1)}), bf16[2048,1024]{1,0:T(8,128)(2,1)}) %all-gather.2.cloned.1.call-update) | async-done | bytes 4194320 | tf_op jit(solution)/shard_map/all_gather | solution.py:124
  95.3 1.3 collective-permute-start
  97.8 0.0 copy-start.3
  97.9 1.4 convert_reduce_fusion.1
  99.3 1.5 fusion.32
  100.8 1.1 multiply_reduce_fusion.2
  101.9 0.1 multiply_convert_fusion.3
  102.1 0.9 copy-done.12
  103.0 1.8 fusion.12
  104.8 0.0 copy-start.15
  104.8 1.3 fusion.45
  106.1 36.2 %collective-permute-done = bf16[2048,1024]{1,0:T(8,128)(2,1)} collective-permute-done((bf16[2048,1024]{1,0:T(8,128)(2,1)}, bf16[2048,1024]{1,0:T(8,128)(2,1)}, u32[]{:S(2)}, u32[]{:S(2)}) %collective-permute-start) | collective-permute-done | bytes 4194336 | tf_op jit(solution)/shard_map/ppermute | solution.py:11
  142.3 3.7 fusion.9
  146.0 0.0 copy-start.7
  146.1 3.9 multiply_reduce_fusion
  150.0 0.3 multiply_convert_fusion.1
  150.3 0.8 copy-done.9
  151.0 2.9 convolution_convert_fusion.1
  153.9 4.7 copy.12
  158.6 0.0 reduce-scatter.16.cloned.1.call-update
  158.6 0.0 reduce-scatter.10.cloned.1.call-start
  158.7 0.0 copy-start.16
  158.7 2.8 multiply_convert_fusion
  161.4 4.7 collective-permute-start.1
  166.1 61.5 %collective-permute-done.1 = bf16[2048,1024]{1,0:T(8,128)(2,1)S(1)} collective-permute-done((bf16[2048,1024]{1,0:T(8,128)(2,1)S(1)}, bf16[2048,1024]{1,0:T(8,128)(2,1)S(1)}, u32[]{:S(2)}, u32[]{:S(2)}) %collective-permute-start.1) | collective-permute-done | bytes 4194336 | tf_op jit(solution)/shard_map/ppermute | solution.py:11
  227.6 3.2 add_convert_fusion
  230.8 0.0 reduce-scatter.10.cloned.1.call-update
  230.9 0.0 reduce-scatter.12.cloned.1.call-start
  230.9 49.7 %reduce-scatter.16.cloned.1.call-done = bf16[128,1536]{1,0:T(8,128)(2,1)} async-done(((bf16[1024,1536]{1,0:T(8,128)(2,1)}), bf16[128,1536]{1,0:T(8,128)(2,1)}) %reduce-scatter.16.cloned.1.call-update) | async-done | bytes 393232
  280.6 1.9 copy.13
  282.5 0.0 reduce-scatter.12.cloned.1.call-update
  282.5 0.0 reduce-scatter.18.cloned.1.call-start
  282.6 90.9 %reduce-scatter.10.cloned.1.call-done = bf16[256,1024]{1,0:T(8,128)(2,1)} async-done(((bf16[2048,1024]{1,0:T(8,128)(2,1)}), bf16[256,1024]{1,0:T(8,128)(2,1)}) %reduce-scatter.10.cloned.1.call-update) | async-done | bytes 524304 | tf_op jit(solution)/shard_map/reduce_scatter | solution.py:143
  373.5 1.8 fusion.34
  375.3 1.3 fusion.36
  376.6 0.8 copy-done.8
  377.4 2.9 convolution_convert_fusion
  380.3 4.6 copy.14
  385.0 0.0 reduce-scatter.18.cloned.1.call-update
  385.0 0.0 reduce-scatter.14.cloned.1.call-start
  385.1 0.0 copy-start.4
  385.1 2.6 fusion.44
  387.7 1.6 fusion.31
  389.3 99.3 %reduce-scatter.12.cloned.1.call-done = bf16[48,128]{1,0:T(8,128)(2,1)} async-done(((bf16[1536,128]{1,0:T(8,128)(2,1)}), bf16[48,128]{1,0:T(8,128)(2,1)}) %reduce-scatter.12.cloned.1.call-update) | async-done | bytes 12304 | tf_op jit(solution)/shard_map/reduce_scatter | solution.py:175
  488.6 1.3 convert_multiply_fusion.2
  489.9 4.5 fusion.43
  494.4 82.8 %reduce-scatter.18.cloned.1.call-done = bf16[128,1536]{1,0:T(8,128)(2,1)} async-done(((bf16[1024,1536]{1,0:T(8,128)(2,1)}), bf16[128,1536]{1,0:T(8,128)(2,1)}) %reduce-scatter.18.cloned.1.call-update) | async-done | bytes 393232
  577.2 1.9 copy.15
  579.2 0.0 reduce-scatter.14.cloned.1.call-update
  579.2 3.3 fusion.26
  582.5 109.4 %reduce-scatter.14.cloned.1.call-done = bf16[48,128]{1,0:T(8,128)(2,1)} async-done(((bf16[1536,128]{1,0:T(8,128)(2,1)}), bf16[48,128]{1,0:T(8,128)(2,1)}) %reduce-scatter.14.cloned.1.call-update) | async-done | bytes 12304 | tf_op jit(solution)/shard_map/reduce_scatter | solution.py:178
  691.9 1.3 convert_multiply_fusion.1
  (30 shorter events, 0.1 us)
Async XLA Ops:
  7.2 93.6 %copy-start = (bf16[1536,1024]{1,0:T(8,128)(2,1)S(1)}, bf16[1536,1024]{1,0:T(8,128)(2,1)}, u32[]{:S(2)}) copy-start(bf16[1536,1024]{1,0:T(8,128)(2,1)} %param.12) | copy-start | bytes 9437188
  7.2 3.0 copy-start.14
  7.2 88.1 %all-gather.2.cloned.1.call-start = ((), (), s32[]{:S(2)}) async-start(), calls=%async_computation.5 | async-start | bytes 4718592 | tf_op jit(solution)/shard_map/all_gather | solution.py:124
  7.2 3.0 copy-start.5
  13.3 1.1 copy-start.1
  14.4 86.4 %copy-start.13 = (f32[1536]{0:T(1024)S(1)}, f32[1536]{0:T(1024)}, u32[]{:S(2)}) copy-start(f32[1536]{0:T(1024)} %param.10) | copy-start | bytes 18436
  15.3 265.3 %reduce-scatter.16.cloned.1.call-start = ((), (), s32[]{:S(2)}) async-start(), calls=%async_computation.9 | async-start | bytes 3538944
  95.3 47.0 %collective-permute-start = (bf16[2048,1024]{1,0:T(8,128)(2,1)}, bf16[2048,1024]{1,0:T(8,128)(2,1)}, u32[]{:S(2)}, u32[]{:S(2)}) collective-permute-start(bf16[2048,1024]{1,0:T(8,128)(2,1)} %all-gather.2.cloned.1.call-done), channel_id=1, source_target_pairs={{0,8},{8,16},{16,24},{24,32},{32,40},{40,48},{48,56},{56,64},{64,7... | collective-permute-start | bytes 12582920 | tf_op jit(solution)/shard_map/ppermute | solution.py:11
  97.8 2.9 copy-start.3
  100.8 2.2 copy-start.12
  102.1 40.2 %copy-start.10 = (bf16[256,1024]{1,0:T(8,128)(2,1)}, bf16[256,1024]{1,0:T(8,128)(2,1)S(1)}, u32[]{:S(2)}) copy-start(bf16[256,1024]{1,0:T(8,128)(2,1)S(1)} %multiply_convert_fusion.3) | copy-start | bytes 1572868
  104.8 1.3 copy-start.15
  146.0 3.9 copy-start.7
  150.3 0.8 copy-start.9
  158.6 214.9 %reduce-scatter.10.cloned.1.call-start = ((), (), s32[]{:S(2)}) async-start(), calls=%async_computation.6 | async-start | bytes 4718592 | tf_op jit(solution)/shard_map/reduce_scatter | solution.py:143
  158.7 69.0 %copy-start.11 = (bf16[256,1024]{1,0:T(8,128)(2,1)S(1)}, bf16[256,1024]{1,0:T(8,128)(2,1)}, u32[]{:S(2)}) copy-start(bf16[256,1024]{1,0:T(8,128)(2,1)} %copy-done.10) | copy-start | bytes 1572868
  158.7 69.0 %copy-start.16 = (bf16[256,2048]{1,0:T(8,128)(2,1)S(1)}, bf16[256,2048]{1,0:T(8,128)(2,1)}, u32[]{:S(2)}) copy-start(bf16[256,2048]{1,0:T(8,128)(2,1)} %copy-done.15) | copy-start | bytes 3145732
  161.4 66.2 %collective-permute-start.1 = (bf16[2048,1024]{1,0:T(8,128)(2,1)S(1)}, bf16[2048,1024]{1,0:T(8,128)(2,1)S(1)}, u32[]{:S(2)}, u32[]{:S(2)}) collective-permute-start(bf16[2048,1024]{1,0:T(8,128)(2,1)S(1)} %multiply_convert_fusion), channel_id=1, source_target_pairs={{0,248},{8,0},{16,8},{24,16},{32,24},{40,32},{48,40},{56,48},{64,5... | collective-permute-start | bytes 12582920 | tf_op jit(solution)/shard_map/ppermute | solution.py:11
  230.9 257.7 %reduce-scatter.12.cloned.1.call-start = ((), (), s32[]{:S(2)}) async-start(), calls=%async_computation.7 | async-start | bytes 405504 | tf_op jit(solution)/shard_map/reduce_scatter | solution.py:175
  282.5 294.7 %reduce-scatter.18.cloned.1.call-start = ((), (), s32[]{:S(2)}) async-start(), calls=%async_computation.10 | async-start | bytes 3538944
  373.5 1.8 copy-start.2
  373.5 3.9 copy-start.6
  376.6 0.8 copy-start.8
  385.0 306.9 %reduce-scatter.14.cloned.1.call-start = ((), (), s32[]{:S(2)}) async-start(), calls=%async_computation.8 | async-start | bytes 405504 | tf_op jit(solution)/shard_map/reduce_scatter | solution.py:178
  385.1 2.6 copy-start.4
Sparse Core Ops, SparseCore 0:
  15.4 79.8 all-gather.1
  158.7 121.8 reduce-scatter.15
  284.7 88.7 reduce-scatter.9
  376.6 111.9 reduce-scatter.11
  492.6 84.6 reduce-scatter.17
  579.6 112.2 reduce-scatter.13
where the time goes:
time: 704 us; the launch traced here: 700 us
  waiting for transfers between devices  610 us (87%)
  matrix products  33.8 us (5%)
  other arithmetic  17.8 us (3%)
  local copies, waits for them, and re-layouts  16.7 us (2%)
  between operations  15.7 us (2%)
    unnamed x8, waiting for transfers between devices  133 us
    reduce_scatter x1, waiting for transfers between devices, on_device(): lax.psum_scatter(inner_txt.astype(jnp.bfloat16), 'blk', scatter_dimension...  109 us
    reduce_scatter x1, waiting for transfers between devices, on_device(): lax.psum_scatter(inner_img.astype(jnp.bfloat16), 'blk', scatter_dimension...  99.3 us
    ppermute x2, waiting for transfers between devices, from_behind(): lax.ppermute(shard, axis, [(i, (i + by) % size) for i in range(size)])  97.7 us
    reduce_scatter x1, waiting for transfers between devices, on_device(): lax.psum_scatter(d_txt_terms.astype(jnp.bfloat16), 'group', scatter_dimen...  90.9 us
    all_gather x1, waiting for transfers between devices, on_device(): lax.all_gather(text_embedding, 'group', axis=0, tiled=True)  79.9 us
    unnamed x38, local copies, waits for them, and re-layouts  16.7 us
  transfers between devices with their start and end apart: 8, of which 8 were waited for; matrix products, arithmetic and copies ran while one was open for 6% of the time, Pallas kernels for 0%

commit v1 on v0

v1 whole, which is shorter than its diff:
```python
import functools
import math

import jax
import jax.numpy as jnp
from jax import lax
from jax.experimental import pallas as pl
from jax.experimental.pallas import tpu as pltpu
from jax.sharding import PartitionSpec as P

BF = jnp.bfloat16
F32 = jnp.float32
NT = (((1,), (1,)), ((), ()))
TN = (((0,), (0,)), ((), ()))


def device_at(x, y, z, c):
    x, y, z = lax.rem(x, 4), lax.rem(y, 4), lax.rem(z, 8)
    return {"blk": z * 4 + lax.rem(x, 2) * 2 + c, "group": y * 2 + x // 2}


def remote(src, dst, send, recv, device):
    return pltpu.make_async_remote_copy(
        src_ref=src,
        dst_ref=dst,
        send_sem=send,
        recv_sem=recv,
        device_id=device,
        device_id_type=pl.DeviceIdType.MESH,
    )


def landed(ref, sem):
    pltpu.make_async_copy(ref, ref, sem).wait()


def kernel(
    scale,
    sharp_ref,
    off_ref,
    gain_i,
    gain_t,
    feat_i,
    feat_t,
    w_i,
    w_t,
    gi_out,
    gt_out,
    wi_out,
    wt_out,
    feats,
    weights,
    gains,
    act,
    act_t,
    unit,
    inv_norm,
    mean_s,
    rstd_s,
    imgs,
    txts,
    coef,
    d_own,
    d_txt,
    di_send,
    di_recv,
    dt_send,
    dt_recv,
    dp,
    d_act,
    wb,
    wr1,
    s1,
    wr2,
    s2,
    wr3,
    fin,
    load_sem,
    i_send,
    i_recv,
    t_send,
    t_recv,
    a_sem,
    di_ss,
    di_rs,
    dt_ss,
    dt_rs,
    dp_sem,
    w1_ss,
    w1_rs,
    w2_ss,
    w2_rs,
    w3_ss,
    w3_rs,
    f_sem,
):
    k = lax.axis_index("blk")
    g = lax.axis_index("group")
    c = lax.rem(k, 2)
    z = k // 4
    xl = lax.rem(k // 2, 2)
    y = g // 2
    xh = lax.rem(g, 2)
    x = 2 * xh + xl
    oc = 1 - c
    ox = 1 - xh
    other = {"blk": k + 1 - 2 * c, "group": g}
    partner = {"blk": k, "group": y * 2 + ox}
    behind = lax.rem(k + 31, 32)
    ahead = lax.rem(k + 1, 32)
    linked = lax.rem(k + 31 + 2 * c, 32)
    rows, width = feats.shape[1], feats.shape[2]
    emb = imgs.shape[2]

    loads = [
        pltpu.make_async_copy(feat_t, feats.at[1], load_sem.at[0]),
        pltpu.make_async_copy(w_t, weights.at[1], load_sem.at[1]),
        pltpu.make_async_copy(feat_i, feats.at[0], load_sem.at[2]),
        pltpu.make_async_copy(w_i, weights.at[0], load_sem.at[3]),
    ]
    for load in loads:
        load.start()

    barrier = pltpu.get_barrier_semaphore()
    partners = [device_at(x, y + d, z, c) for d in (1, 2, 3)]
    partners += [device_at(x + d, y, z, c) for d in (1, 2, 3)]
    partners += [device_at(x, y, z + d, c) for d in range(1, 8)]
    partners += [other]
    partners += [{"blk": linked, "group": y * 2 + j} for j in (0, 1)]
    for device in partners:
        pl.semaphore_signal(
            barrier, inc=1, device_id=device, device_id_type=pl.DeviceIdType.MESH
        )
    gains[0] = gain_i[...]
    gains[1] = gain_t[...]

    step = 32

    def normalize(t, wait_features):
        wait_features.wait()
        place = jnp.where(c == t, 0, 2)

        def body(i, _):
            r = pl.ds(pl.multiple_of(i * step, step), step)
            v = feats[t, r, :].astype(F32)
            mu = jnp.mean(v, axis=-1, keepdims=True)
            cen = v - mu
            rstd = lax.rsqrt(jnp.mean(cen * cen, axis=-1, keepdims=True) + 1e-06)
            mean_s[t, r, :] = mu
            rstd_s[t, r, :] = rstd
            act[place, r, :] = (cen * rstd * gains[t]).astype(BF)
            return 0

        lax.fori_loop(0, rows // step, body, 0)

    def project(t, wait_weights, dst):
        wait_weights.wait()
        place = jnp.where(c == t, 0, 2)
        for n in range(emb // 256):
            cols = slice(n * 256, (n + 1) * 256)
            unit[t, :, cols] = jnp.dot(
                act[place], weights[t, :, cols], preferred_element_type=F32
            )

        def body(i, _):
            r = pl.ds(pl.multiple_of(i * step, step), step)
            p = unit[t, r, :]
            inv = lax.rsqrt(jnp.sum(p * p, axis=-1, keepdims=True) + 1e-06)
            u = p * inv
            unit[t, r, :] = u
            inv_norm[t, r, :] = inv
            dst[r, :] = u.astype(BF)
            return 0

        lax.fori_loop(0, rows // step, body, 0)

    normalize(1, loads[0])
    project(1, loads[1], txts.at[2 + xh])
    pl.semaphore_wait(barrier, 16)

    own_text = txts.at[2 + xh]
    other_text = txts.at[2 + ox]
    t_copies = [
        remote(
            own_text,
            txts.at[xh],
            t_send.at[0],
            t_recv.at[xh],
            {"blk": ahead, "group": g},
        ),
        remote(own_text, txts.at[2 + xh], t_send.at[1], t_recv.at[2], partner),
    ]
    t_copies[1].start()
    t_copies[0].start()
    direct_text = remote(
        own_text,
        txts.at[xh],
        t_send.at[2],
        t_recv.at[xh],
        {"blk": ahead, "group": y * 2 + ox},
    )
    forward_text = remote(
        other_text,
        txts.at[ox],
        t_send.at[2],
        t_recv.at[ox],
        {"blk": ahead, "group": g},
    )

    @pl.when(c == 1)
    def _():
        direct_text.start()

    normalize(0, loads[2])
    project(0, loads[3], imgs.at[0])
    i_copies = [
        remote(
            imgs.at[0],
            imgs.at[d],
            i_send.at[d - 1],
            i_recv.at[d - 1],
            device_at(x, y + d, z, c),
        )
        for d in (1, 3, 2)
    ]
    for copy in i_copies:
        copy.start()
    a_copy = remote(act.at[2], act.at[1], a_sem.at[0], a_sem.at[1], other)
    a_copy.start()

    landed(other_text, t_recv.at[2])

    @pl.when(c == 0)
    def _():
        forward_text.start()

    a_copy.wait()
    for half in (0, 1):
        for n in range(width // 256):
            cols = slice(n * 256, (n + 1) * 256)
            act_t[cols, half * rows : (half + 1) * rows] = act[half, :, cols].T

    landed(txts.at[0], t_recv.at[0])
    landed(txts.at[1], t_recv.at[1])

    sharp = sharp_ref[0]
    off = off_ref[0]
    eye = (
        lax.broadcasted_iota(jnp.int32, (rows, rows), 0)
        == lax.broadcasted_iota(jnp.int32, (rows, rows), 1)
    ).astype(F32)

    def tile(s):
        img = imgs[s]
        for t in range(4):
            sim = lax.dot_general(img, txts[t], NT, preferred_element_type=F32)
            prob = jax.nn.sigmoid(sharp * sim + off)
            if s == 0 and t >= 2:
                prob = prob - eye * (xh == t - 2).astype(F32)
            coef[:, t * rows : (t + 1) * rows] = prob.astype(BF)
        for n in range(emb // 256):
            cols = slice(n * 256, (n + 1) * 256)
            d = jnp.dot(coef[:, 0:rows], txts[0, :, cols], preferred_element_type=F32)
            for t in range(1, 4):
                d += jnp.dot(
                    coef[:, t * rows : (t + 1) * rows],
                    txts[t, :, cols],
                    preferred_element_type=F32,
                )
            if s == 0:
                d_own[:, cols] = d
            else:
                di_send[s - 1, :, cols] = d.astype(BF)
        if s:
            di_copies[s - 1].start()
        for t in range(4):
            ct = coef[:, t * rows : (t + 1) * rows]
            part = lax.dot_general(ct, img, TN, preferred_element_type=F32)
            if s == 0:
                d_txt[t] = part
            else:
                d_txt[t] += part

    di_copies = [
        remote(
            di_send.at[s - 1],
            di_recv.at[s - 1],
            di_ss.at[s - 1],
            di_rs.at[s - 1],
            device_at(x, y + 4 - s, z, c),
        )
        for s in (1, 2, 3)
    ]
    tile(0)
    for s in (1, 3, 2):
        landed(imgs.at[s], i_recv.at[s - 1])
        tile(s)

    dt_copies = []
    for j in (0, 1):
        dt_send[j] = d_txt[j].astype(BF)
        dt_copies.append(
            remote(
                dt_send.at[j],
                dt_recv.at[jnp.where(c == 0, xh, j)],
                dt_ss.at[j],
                dt_rs.at[jnp.where(c == 0, xh, j)],
                {"blk": behind, "group": y * 2 + jnp.where(c == 0, j, xh)},
            )
        )
        dt_copies[j].start()
    dt_copies.append(
        remote(dt_send.at[2], dt_recv.at[2], dt_ss.at[2], dt_rs.at[2], partner)
    )

    @pl.when(c == 0)
    def _():
        landed(dt_recv.at[ox], dt_rs.at[ox])
        dt_send[2] = (d_txt[2 + ox] + dt_recv[ox].astype(F32)).astype(BF)
        dt_copies[2].start()

    @pl.when(c == 1)
    def _():
        dt_send[2] = d_txt[2 + ox].astype(BF)
        dt_copies[2].start()

    def head_backward(t, total):
        place = jnp.where(c == t, 0, 2)

        def body(i, _):
            r = pl.ds(pl.multiple_of(i * step, step), step)
            d = sharp * total(r)
            u = unit[t, r, :]
            dot = jnp.sum(u * d, axis=-1, keepdims=True)
            dp[place, r, :] = ((d - u * dot) * inv_norm[t, r, :]).astype(BF)
            return 0

        lax.fori_loop(0, rows // step, body, 0)

    def img_total(r):
        total = d_own[r, :]
        for s in range(3):
            total += di_recv[s, r, :].astype(F32)
        return total

    for s in range(3):
        landed(di_recv.at[s], di_rs.at[s])
    head_backward(0, img_total)
    dp_copy = remote(dp.at[2], dp.at[1], dp_sem.at[0], dp_sem.at[1], other)

    @pl.when(c == 1)
    def _():
        dp_copy.start()

    landed(dt_recv.at[2], dt_rs.at[2])
    landed(dt_recv.at[xh], dt_rs.at[xh])

    @pl.when(c == 1)
    def _():
        landed(dt_recv.at[ox], dt_rs.at[ox])

    first = jnp.where(c == 0, xh, 0)
    both = c.astype(F32)

    def txt_total(r):
        total = d_txt[2 + xh, r, :] + dt_recv[2, r, :].astype(F32)
        total += dt_recv[first, r, :].astype(F32)
        return total + both * dt_recv[1, r, :].astype(F32)

    head_backward(1, txt_total)

    @pl.when(c == 0)
    def _():
        dp_copy.start()

    landed(dp.at[1], dp_sem.at[1])

    def along_a(d):
        return device_at(
            jnp.where(c == 0, x, x + d), jnp.where(c == 0, y + d, y), z, c
        )

    def along_b(d):
        return device_at(
            jnp.where(c == 0, x + d, x), jnp.where(c == 0, y, y + d), z, c
        )

    pos_a = jnp.where(c == 0, y, x)
    pos_b = jnp.where(c == 0, x, y)

    for n in range(4):
        cols = slice(n * 256, (n + 1) * 256)
        part = jnp.dot(
            act_t[:, 0:rows], dp[0, :, cols], preferred_element_type=F32
        ) + jnp.dot(act_t[:, rows:], dp[1, :, cols], preferred_element_type=F32)
        part = part.astype(BF).reshape(8, 2, 96, 256)
        for xhi in range(2):
            for xlo in range(2):
                px = 2 * xhi + xlo
                wb[jnp.where(c == 0, n, px), jnp.where(c == 0, px, n)] = part[
                    :, xlo, :, xhi * 128 : (xhi + 1) * 128
                ]
    w1 = []
    for d in (2, 1, 3):
        w1.append(
            remote(
                wb.at[lax.rem(pos_a + d, 4)],
                wr1.at[d - 1],
                w1_ss.at[d - 1],
                w1_rs.at[d - 1],
                along_a(d),
            )
        )
        w1[-1].start()

    def features_backward(t, out):
        place = jnp.where(c == t, 0, 2)
        for n in range(width // 256):
            cols = slice(n * 256, (n + 1) * 256)
            d_act[:, cols] = lax.dot_general(
                dp[place], weights[t, cols, :], NT, preferred_element_type=F32
            )

        def body(i, _):
            r = pl.ds(pl.multiple_of(i * step, step), step)
            rstd = rstd_s[t, r, :]
            xhat = (feats[t, r, :].astype(F32) - mean_s[t, r, :]) * rstd
            ghat = d_act[r, :] * gains[t]
            m1 = jnp.mean(ghat, axis=-1, keepdims=True)
            m2 = jnp.mean(ghat * xhat, axis=-1, keepdims=True)
            out[r, :] = rstd * (ghat - m1 - xhat * m2)
            return 0

        lax.fori_loop(0, rows // step, body, 0)

    features_backward(0, gi_out)
    features_backward(1, gt_out)

    for d in (1, 2, 3):
        landed(wr1.at[d - 1], w1_rs.at[d - 1])
    for b in range(4):
        for zz in range(8):
            total = wb[pos_a, b, zz].astype(F32)
            for d in range(3):
                total += wr1[d, b, zz].astype(F32)
            s1[b, zz] = total.astype(BF)
    w2 = []
    for d in (2, 1, 3):
        w2.append(
            remote(
                s1.at[lax.rem(pos_b + d, 4)],
                wr2.at[d - 1],
                w2_ss.at[d - 1],
                w2_rs.at[d - 1],
                along_b(d),
            )
        )
        w2[-1].start()
    for d in (1, 2, 3):
        landed(wr2.at[d - 1], w2_rs.at[d - 1])
    for zz in range(8):
        total = s1[pos_b, zz].astype(F32)
        for d in range(3):
            total += wr2[d, zz].astype(F32)
        s2[zz] = total.astype(BF)
    w3 = []
    for d in (4, 3, 5, 2, 6, 1, 7):
        w3.append(
            remote(
                s2.at[lax.rem(z + d, 8)],
                wr3.at[d - 1],
                w3_ss.at[d - 1],
                w3_rs.at[d - 1],
                device_at(x, y, z + d, c),
            )
        )
        w3[-1].start()
    for d in range(1, 8):
        landed(wr3.at[d - 1], w3_rs.at[d - 1])
    total = s2[z].astype(F32)
    for d in range(7):
        total += wr3[d].astype(F32)
    total = (total * scale).reshape(2, 48, 128)
    fin[2] = total[0]
    fin[3] = total[1]
    f_copy = remote(fin.at[2 + oc], fin.at[c], f_sem.at[0], f_sem.at[1], other)
    f_copy.start()
    landed(fin.at[oc], f_sem.at[1])
    mine = fin[2 + c]
    theirs = fin[oc]
    wi_out[...] = jnp.where(c == 0, mine, theirs)
    wt_out[...] = jnp.where(c == 0, theirs, mine)

    for copy in t_copies + [direct_text] + i_copies + di_copies + dt_copies:
        copy.wait_send()
    for copy in w1 + w2 + w3 + [dp_copy, f_copy]:
        copy.wait_send()


def on_device(feat_i, feat_t, gain_i, gain_t, w_i, w_t, sharp, off):
    rows, width = feat_i.shape
    emb = w_i.shape[1]
    batch = rows * lax.axis_size("group") * lax.axis_size("blk")
    scale = math.sqrt(emb / batch)
    vmem = pl.BlockSpec(memory_space=pltpu.VMEM)
    smem = pl.BlockSpec(memory_space=pltpu.SMEM)
    hbm = pl.BlockSpec(memory_space=pl.ANY)
    dma = pltpu.SemaphoreType.DMA
    return pl.pallas_call(
        functools.partial(kernel, scale),
        name="siglip_grads",
        out_shape=(
            jax.ShapeDtypeStruct((rows, width), F32),
            jax.ShapeDtypeStruct((rows, width), F32),
            jax.ShapeDtypeStruct((48, 128), F32),
            jax.ShapeDtypeStruct((48, 128), F32),
        ),
        in_specs=[smem, smem, vmem, vmem, hbm, hbm, hbm, hbm],
        out_specs=(vmem, vmem, vmem, vmem),
        scratch_shapes=[
            pltpu.VMEM((2, rows, width), BF),
            pltpu.VMEM((2, width, emb), BF),
            pltpu.VMEM((2, 1, width), F32),
            pltpu.VMEM((3, rows, width), BF),
            pltpu.VMEM((width, 2 * rows), BF),
            pltpu.VMEM((2, rows, emb), F32),
            pltpu.VMEM((2, rows, 1), F32),
            pltpu.VMEM((2, rows, 1), F32),
            pltpu.VMEM((2, rows, 1), F32),
            pltpu.VMEM((4, rows, emb), BF),
            pltpu.VMEM((4, rows, emb), BF),
            pltpu.VMEM((rows, 4 * rows), BF),
            pltpu.VMEM((rows, emb), F32),
            pltpu.VMEM((4, rows, emb), F32),
            pltpu.VMEM((3, rows, emb), BF),
            pltpu.VMEM((3, rows, emb), BF),
            pltpu.VMEM((3, rows, emb), BF),
            pltpu.VMEM((3, rows, emb), BF),
            pltpu.VMEM((3, rows, emb), BF),
            pltpu.VMEM((rows, width), F32),
            pltpu.VMEM((4, 4, 8, 96, 128), BF),
            pltpu.VMEM((3, 4, 8, 96, 128), BF),
            pltpu.VMEM((4, 8, 96, 128), BF),
            pltpu.VMEM((3, 8, 96, 128), BF),
            pltpu.VMEM((8, 96, 128), BF),
            pltpu.VMEM((7, 96, 128), BF),
            pltpu.VMEM((4, 48, 128), F32),
            dma((4,)),
            dma((3,)),
            dma((3,)),
            dma((3,)),
            dma((3,)),
            dma((2,)),
            dma((3,)),
            dma((3,)),
            dma((3,)),
            dma((3,)),
            dma((2,)),
            dma((3,)),
            dma((3,)),
            dma((3,)),
            dma((3,)),
            dma((7,)),
            dma((7,)),
            dma((2,)),
        ],
        compiler_params=pltpu.CompilerParams(
            collective_id=0, has_side_effects=True, vmem_limit_bytes=60 << 20
        ),
        cost_estimate=pl.CostEstimate(
            flops=11 * 10**9, bytes_accessed=11 * 10**6, transcendentals=10**6
        ),
    )(
        sharp,
        off,
        gain_i.reshape(1, width),
        gain_t.reshape(1, width),
        feat_i,
        feat_t,
        w_i,
        w_t,
    )


def solution(mesh):
    rows = P(("blk", "group"), None)
    return jax.shard_map(
        on_device,
        mesh=mesh,
        in_specs=(rows, rows, P(), P(), P(), P(), P(), P()),
        out_specs=(rows, rows, P("blk", "group"), P("blk", "group")),
        check_vma=False,
    )
```

time: 704 us -> 116 us (0.16)
  waiting for transfers between devices: 610 us -> 0 us
  Pallas kernels: 0 us -> 106 us
  matrix products: 33.8 us -> 0 us
  other arithmetic: 17.8 us -> 0 us
  between operations: 15.7 us -> 1.95 us
  local copies, waits for them, and re-layouts: 16.7 us -> 7.73 us
    reduce_scatter x3 -> x0, waiting for transfers between devices: 300 us -> none  [the longest x1 109 us: on_device(): lax.psum_scatter(inner_txt.astype(jnp.bfloat16), 'blk', scatter_dimension...]
    unnamed x8 -> x0, waiting for transfers between devices: 133 us -> none
    pallas_call x0 -> x1, Pallas kernels: none -> 106 us  [on_device(): pl.pallas_call(functools.partial(kernel, scale), name='siglip_grads', out...]
    ppermute x2 -> x0, waiting for transfers between devices: 97.7 us -> none  [from_behind(): lax.ppermute(shard, axis, [(i, (i + by) % size) for i in range(size)])]
    all_gather x1 -> x0, waiting for transfers between devices: 79.9 us -> none  [on_device(): lax.all_gather(text_embedding, 'group', axis=0, tiled=True)]
    dot_general x12 -> x0, matrix products: 33.8 us -> none  [the longest x2 7.11 us: projection_backward(): jnp.dot(dproj, projection_weight.T, preferred_element_type=jnp.float32)]
    unnamed x38 -> x10, local copies, waits for them, and re-layouts: 16.7 us -> 5.14 us
    reduce_sum x5 -> x0, other arithmetic: 7.61 us -> none  [the longest x2 2.96 us: projection_forward(): jnp.mean(centered_input * centered_input, axis=-1, keepdims=True) + 1e-06]
  transfers between devices with their start and end apart: 8 -> 0, of which waited for: 8 -> 0; matrix products, arithmetic and copies ran while one was open for 6% -> 0% of each run, Pallas kernels for 0% -> 0%
where the time goes in v1:
time: 116 us; the launch traced here: 115 us
  Pallas kernels  106 us (91%)
  local copies, waits for them, and re-layouts  7.73 us (7%)
  between operations  1.95 us (2%)
    pallas_call x1, Pallas kernels, on_device(): pl.pallas_call(functools.partial(kernel, scale), name='siglip_grads', out...  106 us
    unnamed x10, local copies, waits for them, and re-layouts  5.14 us

profile of v1, /device:TPU:1, one launch (start us, length us, event | category | flops | bytes accessed | tf_op | source)
XLA Modules:
  0.0 115.3 jit_solution(8683385644700845170)
XLA Ops:
  1.9 1.3 %reshape.14.gain_i = f32[1,1536]{1,0:T(1,128)} reshape(f32[1536]{0:T(1024)} %param.10) | data formatting | bytes 12288 | tf_op jit(solution)/shard_map/reshape | solution.py:576
  3.2 1.3 %reshape.15.gain_t = f32[1,1536]{1,0:T(1,128)} reshape(f32[1536]{0:T(1024)} %param.11) | data formatting | bytes 12288 | tf_op jit(solution)/shard_map/reshape | solution.py:577
  4.5 105.7 %siglip_grads.1 = (f32[256,1536]{1,0:T(8,128)}, f32[256,1536]{1,0:T(8,128)}, f32[48,128]{1,0:T(8,128)}, f32[48,128]{1,0:T(8,128)}) custom-call(f32[1]{0:T(128)S(6)} %copy.16.sharp_ref, f32[1]{0:T(128)S(6)} %copy.17.off_ref, f32[1,1536]{1,0:T(1,128)} %reshape.14.gain_i, f32[1,1536]{1,0:T(1,128)} %reshape.15.gain_t, bf16[256,1536]{1,0:T(8,128)(2,1)} %feat_i.1, ...), custom_call_target="tpu_custom_call" | custom-call | flops 11000000512 | bytes 11000000 | tf_op jit(solution)/shard_map/siglip_grads/pallas_call | solution.py:509
  110.2 0.0 copy-start
  110.2 2.8 %copy.18 = f32[256,1536]{1,0:T(8,128)} copy(f32[256,1536]{1,0:T(8,128)} %get-tuple-element.8) | data formatting | bytes 3145728
  113.0 0.0 copy-done
  113.0 0.0 copy-start.2
  113.0 0.0 copy-start.1
  113.0 1.1 copy.19
  114.1 0.0 copy-done.2
  114.1 0.6 copy.20
  114.7 0.0 copy-done.1
  114.7 0.6 copy.21
Async XLA Ops:
  110.2 2.8 %copy-start = (f32[256,1536]{1,0:T(8,128)S(1)}, f32[256,1536]{1,0:T(8,128)}, u32[]{:S(2)}) copy-start(f32[256,1536]{1,0:T(8,128)} %get-tuple-element.9) | copy-start | bytes 4718596
  113.0 1.1 copy-start.2
  113.0 1.8 %copy-start.1 = (f32[48,128]{1,0:T(8,128)S(1)}, f32[48,128]{1,0:T(8,128)}, u32[]{:S(2)}) copy-start(f32[48,128]{1,0:T(8,128)} %get-tuple-element.11) | copy-start | bytes 73732

commit v2 on v1

--- a/solution.py
+++ b/solution.py
@@ -64,17 +64,18 @@
     d_txt,
     di_send,
     di_recv,
+    di_pass,
     dt_send,
     dt_recv,
     dp,
     d_act,
     wb,
+    w_pass,
     wr1,
     s1,
     wr2,
     s2,
     wr3,
-    fin,
     load_sem,
     i_send,
     i_recv,
@@ -92,7 +93,6 @@
     w2_rs,
     w3_ss,
     w3_rs,
-    f_sem,
 ):
     k = lax.axis_index("blk")
     g = lax.axis_index("group")
@@ -125,14 +125,14 @@
     partners = [device_at(x, y + d, z, c) for d in (1, 2, 3)]
     partners += [device_at(x + d, y, z, c) for d in (1, 2, 3)]
     partners += [device_at(x, y, z + d, c) for d in range(1, 8)]
-    partners += [other]
+    partners += [device_at(x, y, z + d, oc) for d in range(8)]
     partners += [{"blk": linked, "group": y * 2 + j} for j in (0, 1)]
     for device in partners:
         pl.semaphore_signal(
             barrier, inc=1, device_id=device, device_id_type=pl.DeviceIdType.MESH
         )
-    gains[0] = gain_i[...]
-    gains[1] = gain_t[...]
+    gains[0] = gain_i[...].reshape(1, width)
+    gains[1] = gain_t[...].reshape(1, width)
 
     step = 32
 
@@ -176,7 +176,7 @@
 
     normalize(1, loads[0])
     project(1, loads[1], txts.at[2 + xh])
-    pl.semaphore_wait(barrier, 16)
+    pl.semaphore_wait(barrier, 23)
 
     own_text = txts.at[2 + xh]
     other_text = txts.at[2 + ox]
@@ -190,7 +190,6 @@
         ),
         remote(own_text, txts.at[2 + xh], t_send.at[1], t_recv.at[2], partner),
     ]
-    t_copies[1].start()
     t_copies[0].start()
     direct_text = remote(
         own_text,
@@ -211,94 +210,79 @@
     def _():
         direct_text.start()
 
+    t_copies[1].start()
     normalize(0, loads[2])
     project(0, loads[3], imgs.at[0])
+    half_a, half_b = pl.ds(0, rows // 2), pl.ds(rows // 2, rows // 2)
+    up, down = device_at(x, y + 1, z, c), device_at(x, y + 3, z, c)
     i_copies = [
         remote(
-            imgs.at[0],
-            imgs.at[d],
-            i_send.at[d - 1],
-            i_recv.at[d - 1],
-            device_at(x, y + d, z, c),
+            imgs.at[src, part], imgs.at[dst, part], i_send.at[n], i_recv.at[n], device
         )
-        for d in (1, 3, 2)
+        for n, (src, dst, part, device) in enumerate(
+            (
+                (0, 1, half_a, up),
+                (0, 1, half_b, up),
+                (0, 3, half_b, down),
+                (0, 3, half_a, down),
+                (1, 2, half_a, up),
+                (3, 2, half_b, down),
+            )
+        )
     ]
-    for copy in i_copies:
-        copy.start()
+    for n in (0, 2, 1, 3):
+        i_copies[n].start()
     a_copy = remote(act.at[2], act.at[1], a_sem.at[0], a_sem.at[1], other)
     a_copy.start()
 
-    landed(other_text, t_recv.at[2])
-
-    @pl.when(c == 0)
-    def _():
-        forward_text.start()
-
-    a_copy.wait()
-    for half in (0, 1):
-        for n in range(width // 256):
-            cols = slice(n * 256, (n + 1) * 256)
-            act_t[cols, half * rows : (half + 1) * rows] = act[half, :, cols].T
-
-    landed(txts.at[0], t_recv.at[0])
-    landed(txts.at[1], t_recv.at[1])
-
     sharp = sharp_ref[0]
     off = off_ref[0]
-    eye = (
-        lax.broadcasted_iota(jnp.int32, (rows, rows), 0)
-        == lax.broadcasted_iota(jnp.int32, (rows, rows), 1)
-    ).astype(F32)
-
-    def tile(s):
+    own, late = 2 + xh, 2 + ox
+
+    def pair(s, t, matching=False, fresh=False):
         img = imgs[s]
-        for t in range(4):
-            sim = lax.dot_general(img, txts[t], NT, preferred_element_type=F32)
-            prob = jax.nn.sigmoid(sharp * sim + off)
-            if s == 0 and t >= 2:
-                prob = prob - eye * (xh == t - 2).astype(F32)
-            coef[:, t * rows : (t + 1) * rows] = prob.astype(BF)
+        sim = lax.dot_general(img, txts[t], NT, preferred_element_type=F32)
+        prob = jax.nn.sigmoid(sharp * sim + off)
+        if matching:
+            row = lax.broadcasted_iota(jnp.int32, (rows, rows), 0)
+            col = lax.broadcasted_iota(jnp.int32, (rows, rows), 1)
+            prob = prob - (row == col).astype(F32)
+        chosen = prob.astype(BF)
+        coef[s, t] = chosen
+        part = lax.dot_general(chosen, img, TN, preferred_element_type=F32)
+        if fresh:
+            d_txt[t] = part
+        else:
+            d_txt[t] += part
+
+    def image_terms(s, dst):
         for n in range(emb // 256):
             cols = slice(n * 256, (n + 1) * 256)
-            d = jnp.dot(coef[:, 0:rows], txts[0, :, cols], preferred_element_type=F32)
+            d = jnp.dot(coef[s, 0], txts[0, :, cols], preferred_element_type=F32)
             for t in range(1, 4):
-                d += jnp.dot(
-                    coef[:, t * rows : (t + 1) * rows],
-                    txts[t, :, cols],
-                    preferred_element_type=F32,
-                )
-            if s == 0:
-                d_own[:, cols] = d
-            else:
-                di_send[s - 1, :, cols] = d.astype(BF)
-        if s:
-            di_copies[s - 1].start()
-        for t in range(4):
-            ct = coef[:, t * rows : (t + 1) * rows]
-            part = lax.dot_general(ct, img, TN, preferred_element_type=F32)
-            if s == 0:
-                d_txt[t] = part
-            else:
-                d_txt[t] += part
-
+                d += jnp.dot(coef[s, t], txts[t, :, cols], preferred_element_type=F32)
+            dst[:, cols] = d.astype(dst.dtype)
+
+    quarters = [pl.ds(n * rows // 4, rows // 4) for n in range(4)]
     di_copies = [
-        remote(
-            di_send.at[s - 1],
-            di_recv.at[s - 1],
-            di_ss.at[s - 1],
-            di_rs.at[s - 1],
-            device_at(x, y + 4 - s, z, c),
+        remote(src, dst, di_ss.at[n], di_rs.at[n], device)
+        for n, (src, dst, device) in enumerate(
+            (
+                (di_send.at[2, half_b], di_recv.at[0, half_b], up),
+                (di_send.at[1, quarters[0]], di_pass.at[quarters[0]], up),
+                (di_send.at[1, quarters[1]], di_pass.at[quarters[1]], up),
+                (di_send.at[2, quarters[0]], di_recv.at[0, quarters[0]], up),
+                (di_send.at[2, quarters[1]], di_recv.at[0, quarters[1]], up),
+                (di_send.at[0, half_a], di_recv.at[1, half_a], down),
+                (di_send.at[1, quarters[2]], di_pass.at[quarters[2]], down),
+                (di_send.at[1, quarters[3]], di_pass.at[quarters[3]], down),
+                (di_send.at[0, quarters[2]], di_recv.at[1, quarters[2]], down),
+                (di_send.at[0, quarters[3]], di_recv.at[1, quarters[3]], down),
+            )
         )
-        for s in (1, 2, 3)
     ]
-    tile(0)
-    for s in (1, 3, 2):
-        landed(imgs.at[s], i_recv.at[s - 1])
-        tile(s)
-
     dt_copies = []
     for j in (0, 1):
-        dt_send[j] = d_txt[j].astype(BF)
         dt_copies.append(
             remote(
                 dt_send.at[j],
@@ -308,10 +292,71 @@
                 {"blk": behind, "group": y * 2 + jnp.where(c == 0, j, xh)},
             )
         )
-        dt_copies[j].start()
     dt_copies.append(
         remote(dt_send.at[2], dt_recv.at[2], dt_ss.at[2], dt_rs.at[2], partner)
     )
+
+    pair(0, own, matching=True, fresh=True)
+    a_copy.wait()
+    for half in (0, 1):
+        for n in range(width // 256):
+            cols = slice(n * 256, (n + 1) * 256)
+            act_t[cols, half * rows : (half + 1) * rows] = act[half, :, cols].T
+    landed(txts.at[xh], t_recv.at[xh])
+    pair(0, xh, fresh=True)
+    i_copies[0].wait_recv()
+    i_copies[4].start()
+    i_copies[2].wait_recv()
+    i_copies[5].start()
+
+    @pl.when(c == 0)
+    def _():
+        landed(txts.at[ox], t_recv.at[ox])
+        pair(0, ox, fresh=True)
+
+    i_copies[1].wait_recv()
+    i_copies[3].wait_recv()
+    for s in (3, 1):
+        pair(s, own)
+        pair(s, xh)
+
+    @pl.when(c == 0)
+    def _():
+        pair(3, ox)
+        pair(1, ox)
+
+    landed(other_text, t_recv.at[2])
+
+    @pl.when(c == 0)
+    def _():
+        forward_text.start()
+
+    @pl.when(c == 1)
+    def _():
+        landed(txts.at[ox], t_recv.at[ox])
+        pair(0, ox, fresh=True)
+        pair(3, ox)
+        pair(1, ox)
+
+    pair(3, late, fresh=True)
+    image_terms(3, di_send.at[2])
+    di_copies[0].start()
+    pair(1, late)
+    image_terms(1, di_send.at[0])
+    di_copies[5].start()
+    i_copies[4].wait_recv()
+    i_copies[5].wait_recv()
+    pair(2, xh)
+    pair(2, ox)
+    for j in (0, 1):
+        dt_send[j] = d_txt[j].astype(BF)
+        dt_copies[j].start()
+    pair(2, late)
+    pair(2, own)
+    image_terms(2, di_send.at[1])
+    for n in (1, 6, 2, 7):
+        di_copies[n].start()
+    pair(0, late)
 
     @pl.when(c == 0)
     def _():
@@ -339,12 +384,21 @@
 
     def img_total(r):
         total = d_own[r, :]
-        for s in range(3):
-            total += di_recv[s, r, :].astype(F32)
+        for n in range(2):
+            total += di_recv[n, r, :].astype(F32)
         return total
 
-    for s in range(3):
-        landed(di_recv.at[s], di_rs.at[s])
+    image_terms(0, d_own)
+    for n, slot in ((0, 2), (2, 0), (1, 2), (3, 0)):
+        arrived, onward = ((1, 3), (2, 4), (6, 8), (7, 9))[n]
+        di_copies[arrived].wait_recv()
+        di_send[slot, quarters[n], :] = (
+            di_send[slot, quarters[n], :].astype(F32)
+            + di_pass[quarters[n], :].astype(F32)
+        ).astype(BF)
+        di_copies[onward].start()
+    for n in (0, 5, 3, 8, 4, 9):
+        di_copies[n].wait_recv()
     head_backward(0, img_total)
     dp_copy = remote(dp.at[2], dp.at[1], dp_sem.at[0], dp_sem.at[1], other)
 
@@ -380,38 +434,45 @@
             jnp.where(c == 0, x, x + d), jnp.where(c == 0, y + d, y), z, c
         )
 
-    def along_b(d):
-        return device_at(
-            jnp.where(c == 0, x + d, x), jnp.where(c == 0, y, y + d), z, c
-        )
-
     pos_a = jnp.where(c == 0, y, x)
     pos_b = jnp.where(c == 0, x, y)
-
-    for n in range(4):
-        cols = slice(n * 256, (n + 1) * 256)
+    fore, aft, far = (lax.rem(pos_a + d, 4) for d in (1, 3, 2))
+
+    pieces = (
+        [(wb.at[far, b], w_pass.at[b], along_a(1)) for b in (0, 1)]
+        + [(wb.at[fore, b], wr1.at[0, b], along_a(1)) for b in (2, 3, 0, 1)]
+        + [(wb.at[far, b], w_pass.at[b], along_a(3)) for b in (2, 3)]
+        + [(wb.at[aft, b], wr1.at[1, b], along_a(3)) for b in (0, 1, 2, 3)]
+    )
+    w1 = [
+        remote(src, dst, w1_ss.at[n], w1_rs.at[n], device)
+        for n, (src, dst, device) in enumerate(pieces)
+    ]
+
+    for j in range(4):
+        by_text = (0, 2, 1, 3)[j]
+        n = jnp.where(c == 0, lax.rem(y + (2, 1, 3, 0)[j], 4), by_text)
+        cols = pl.ds(pl.multiple_of(n * 256, 256), 256)
         part = jnp.dot(
             act_t[:, 0:rows], dp[0, :, cols], preferred_element_type=F32
         ) + jnp.dot(act_t[:, rows:], dp[1, :, cols], preferred_element_type=F32)
-        part = part.astype(BF).reshape(8, 2, 96, 256)
+        part = part.astype(BF).reshape(8, 2, 2, 48, 256)
         for xhi in range(2):
             for xlo in range(2):
                 px = 2 * xhi + xlo
                 wb[jnp.where(c == 0, n, px), jnp.where(c == 0, px, n)] = part[
-                    :, xlo, :, xhi * 128 : (xhi + 1) * 128
+                    :, xlo, :, :, xhi * 128 : (xhi + 1) * 128
                 ]
-    w1 = []
-    for d in (2, 1, 3):
-        w1.append(
-            remote(
-                wb.at[lax.rem(pos_a + d, 4)],
-                wr1.at[d - 1],
-                w1_ss.at[d - 1],
-                w1_rs.at[d - 1],
-                along_a(d),
-            )
-        )
-        w1[-1].start()
+
+        @pl.when(c == 0)
+        def _():
+            for n in ((0, 6, 1, 7), (2, 3), (8, 9), ())[j]:
+                w1[n].start()
+
+        @pl.when(c == 1)
+        def _():
+            for n in ((0, 8), (6, 2), (1, 9), (7, 3))[j]:
+                w1[n].start()
 
     def features_backward(t, out):
         place = jnp.where(c == t, 0, 2)
@@ -434,67 +495,106 @@
         lax.fori_loop(0, rows // step, body, 0)
 
     features_backward(0, gi_out)
+    for b, arrived, onward, chunk in (
+        (0, 0, 4, fore),
+        (2, 6, 10, aft),
+        (1, 1, 5, fore),
+        (3, 7, 11, aft),
+    ):
+        w1[arrived].wait_recv()
+        for zz in range(8):
+            wb[chunk, b, zz] = (
+                wb[chunk, b, zz].astype(F32) + w_pass[b, zz].astype(F32)
+            ).astype(BF)
+        w1[onward].start()
     features_backward(1, gt_out)
 
-    for d in (1, 2, 3):
-        landed(wr1.at[d - 1], w1_rs.at[d - 1])
-    for b in range(4):
+    def w2_copy(b, slot, half, device):
+        part = pl.ds(half * 4, 4)
+        return remote(
+            s1.at[b, part],
+            wr2.at[slot, part],
+            w2_ss.at[slot, half],
+            w2_rs.at[slot, half],
+            device,
+        )
+
+    for b, early, late_piece in ((0, 8, 4), (2, 2, 10), (1, 9, 5), (3, 3, 11)):
+        w1[early].wait_recv()
+        w1[late_piece].wait_recv()
         for zz in range(8):
-            total = wb[pos_a, b, zz].astype(F32)
+            total = wb[pos_a, b, zz].astype(F32) + wr1[0, b, zz].astype(F32)
+            s1[b, zz] = (total + wr1[1, b, zz].astype(F32)).astype(BF)
+
+        @pl.when(pos_b != b)
+        def _():
+            for half in (0, 1):
+                w2_copy(
+                    b,
+                    lax.rem(b + 3 - pos_b, 4),
+                    half,
+                    device_at(jnp.where(c == 0, b, x), jnp.where(c == 0, y, b), z, c),
+                ).start()
+
+    def w3_copy(zd, cd):
+        return remote(
+            s2.at[zd, cd],
+            wr3.at[c, z],
+            w3_ss.at[zd, cd],
+            w3_rs.at[c, z],
+            {"blk": zd * 4 + xl * 2 + cd, "group": g},
+        )
+
+    for half in (0, 1):
+        for d in range(3):
+            w2_copy(0, d, half, other).wait_recv()
+        for zd in range(half * 4, half * 4 + 4):
+            total = s1[pos_b, zd].astype(F32)
             for d in range(3):
-                total += wr1[d, b, zz].astype(F32)
-            s1[b, zz] = total.astype(BF)
-    w2 = []
-    for d in (2, 1, 3):
-        w2.append(
-            remote(
-                s1.at[lax.rem(pos_b + d, 4)],
-                wr2.at[d - 1],
-                w2_ss.at[d - 1],
-                w2_rs.at[d - 1],
-                along_b(d),
-            )
-        )
-        w2[-1].start()
-    for d in (1, 2, 3):
-        landed(wr2.at[d - 1], w2_rs.at[d - 1])
-    for zz in range(8):
-        total = s1[pos_b, zz].astype(F32)
-        for d in range(3):
-            total += wr2[d, zz].astype(F32)
-        s2[zz] = total.astype(BF)
-    w3 = []
-    for d in (4, 3, 5, 2, 6, 1, 7):
-        w3.append(
-            remote(
-                s2.at[lax.rem(z + d, 8)],
-                wr3.at[d - 1],
-                w3_ss.at[d - 1],
-                w3_rs.at[d - 1],
-                device_at(x, y, z + d, c),
-            )
-        )
-        w3[-1].start()
-    for d in range(1, 8):
-        landed(wr3.at[d - 1], w3_rs.at[d - 1])
-    total = s2[z].astype(F32)
-    for d in range(7):
-        total += wr3[d].astype(F32)
-    total = (total * scale).reshape(2, 48, 128)
-    fin[2] = total[0]
-    fin[3] = total[1]
-    f_copy = remote(fin.at[2 + oc], fin.at[c], f_sem.at[0], f_sem.at[1], other)
-    f_copy.start()
-    landed(fin.at[oc], f_sem.at[1])
-    mine = fin[2 + c]
-    theirs = fin[oc]
-    wi_out[...] = jnp.where(c == 0, mine, theirs)
-    wt_out[...] = jnp.where(c == 0, theirs, mine)
+                total += wr2[d, zd].astype(F32)
+            s2[zd] = total.astype(BF)
+            for cd in (0, 1):
+
+                @pl.when((zd != z) | (cd != c))
+                def _():
+                    w3_copy(zd, cd).start()
+
+    wr3[c, z] = s2[z, c]
+    for t, out in ((0, wi_out), (1, wt_out)):
+        for zs in range(8):
+
+            @pl.when((zs != z) | (t != c))
+            def _():
+                landed(wr3.at[t, zs], w3_rs.at[t, zs])
+
+        total = wr3[t, 0].astype(F32)
+        for zs in range(1, 8):
+            total += wr3[t, zs].astype(F32)
+        out[...] = total * scale
 
     for copy in t_copies + [direct_text] + i_copies + di_copies + dt_copies:
         copy.wait_send()
-    for copy in w1 + w2 + w3 + [dp_copy, f_copy]:
+    for copy in w1 + [dp_copy]:
         copy.wait_send()
+    for half in (0, 1):
+        for d in range(3):
+            w2_copy(0, d, half, other).wait_send()
+    for zd in range(8):
+        for cd in (0, 1):
+
+            @pl.when((zd != z) | (cd != c))
+            def _():
+                w3_copy(zd, cd).wait_send()
+
+
+def hand_out(*refs):
+    copies = [
+        pltpu.make_async_copy(refs[n], refs[4 + n], refs[8].at[n]) for n in range(4)
+    ]
+    for copy in copies:
+        copy.start()
+    for copy in copies:
+        copy.wait()
 
 
 def on_device(feat_i, feat_t, gain_i, gain_t, w_i, w_t, sharp, off):
@@ -506,14 +606,14 @@
     smem = pl.BlockSpec(memory_space=pltpu.SMEM)
     hbm = pl.BlockSpec(memory_space=pl.ANY)
     dma = pltpu.SemaphoreType.DMA
-    return pl.pallas_call(
+    grads = pl.pallas_call(
         functools.partial(kernel, scale),
         name="siglip_grads",
         out_shape=(
-            jax.ShapeDtypeStruct((rows, width), F32),
-            jax.ShapeDtypeStruct((rows, width), F32),
-            jax.ShapeDtypeStruct((48, 128), F32),
-            jax.ShapeDtypeStruct((48, 128), F32),
+            pltpu.VMEM((rows, width), F32),
+            pltpu.VMEM((rows, width), F32),
+            pltpu.VMEM((48, 128), F32),
+            pltpu.VMEM((48, 128), F32),
         ),
         in_specs=[smem, smem, vmem, vmem, hbm, hbm, hbm, hbm],
         out_specs=(vmem, vmem, vmem, vmem),
@@ -529,43 +629,43 @@
             pltpu.VMEM((2, rows, 1), F32),
             pltpu.VMEM((4, rows, emb), BF),
             pltpu.VMEM((4, rows, emb), BF),
-            pltpu.VMEM((rows, 4 * rows), BF),
+            pltpu.VMEM((4, 4, rows, rows), BF),
             pltpu.VMEM((rows, emb), F32),
             pltpu.VMEM((4, rows, emb), F32),
             pltpu.VMEM((3, rows, emb), BF),
-            pltpu.VMEM((3, rows, emb), BF),
+            pltpu.VMEM((2, rows, emb), BF),
+            pltpu.VMEM((rows, emb), BF),
             pltpu.VMEM((3, rows, emb), BF),
             pltpu.VMEM((3, rows, emb), BF),
             pltpu.VMEM((3, rows, emb), BF),
             pltpu.VMEM((rows, width), F32),
-            pltpu.VMEM((4, 4, 8, 96, 128), BF),
-            pltpu.VMEM((3, 4, 8, 96, 128), BF),
-            pltpu.VMEM((4, 8, 96, 128), BF),
-            pltpu.VMEM((3, 8, 96, 128), BF),
-            pltpu.VMEM((8, 96, 128), BF),
-            pltpu.VMEM((7, 96, 128), BF),
-            pltpu.VMEM((4, 48, 128), F32),
+            pltpu.VMEM((4, 4, 8, 2, 48, 128), BF),
+            pltpu.VMEM((4, 8, 2, 48, 128), BF),
+            pltpu.VMEM((2, 4, 8, 2, 48, 128), BF),
+            pltpu.VMEM((4, 8, 2, 48, 128), BF),
+            pltpu.VMEM((3, 8, 2, 48, 128), BF),
+            pltpu.VMEM((8, 2, 48, 128), BF),
+            pltpu.VMEM((2, 8, 48, 128), BF),
             dma((4,)),
-            dma((3,)),
-            dma((3,)),
+            dma((6,)),
+            dma((6,)),
             dma((3,)),
             dma((3,)),
             dma((2,)),
-            dma((3,)),
-            dma((3,)),
+            dma((10,)),
+            dma((10,)),
             dma((3,)),
             dma((3,)),
             dma((2,)),
-            dma((3,)),
-            dma((3,)),
-            dma((3,)),
-            dma((3,)),
-            dma((7,)),
-            dma((7,)),
-            dma((2,)),
+            dma((12,)),
+            dma((12,)),
+            dma((3, 2)),
+            dma((3, 2)),
+            dma((8, 2)),
+            dma((2, 8)),
         ],
         compiler_params=pltpu.CompilerParams(
-            collective_id=0, has_side_effects=True, vmem_limit_bytes=60 << 20
+            collective_id=0, has_side_effects=True, vmem_limit_bytes=54 << 20
         ),
         cost_estimate=pl.CostEstimate(
             flops=11 * 10**9, bytes_accessed=11 * 10**6, transcendentals=10**6
@@ -573,13 +673,22 @@
     )(
         sharp,
         off,
-        gain_i.reshape(1, width),
-        gain_t.reshape(1, width),
+        gain_i,
+        gain_t,
         feat_i,
         feat_t,
         w_i,
         w_t,
     )
+    return pl.pallas_call(
+        hand_out,
+        name="hand_out",
+        out_shape=tuple(jax.ShapeDtypeStruct(a.shape, a.dtype) for a in grads),
+        in_specs=[hbm] * 4,
+        out_specs=(hbm,) * 4,
+        scratch_shapes=[dma((4,))],
+        compiler_params=pltpu.CompilerParams(vmem_limit_bytes=1 << 20),
+    )(*grads)
 
 
 def solution(mesh):

time: 116 us -> 100 us (0.86)
  the two profiles are of different devices: /device:TPU:1 before, /device:TPU:25 now
where the time goes in v2:
time: 100 us; the launch traced here: 99.8 us
  Pallas kernels  97.8 us (98%)
  between operations  2.09 us (2%)
    pallas_call x1, Pallas kernels, on_device(): pl.pallas_call(functools.partial(kernel, scale), name='siglip_grads', out...  96 us

profile of v2, /device:TPU:25, one launch (start us, length us, event | category | flops | bytes accessed | tf_op | source)
XLA Modules:
  0.0 99.8 jit_solution(9357870369064952720)
XLA Ops:
  1.9 96.0 %siglip_grads.1 = (f32[256,1536]{1,0:T(8,128)S(1)}, f32[256,1536]{1,0:T(8,128)S(1)}, f32[48,128]{1,0:T(8,128)S(1)}, f32[48,128]{1,0:T(8,128)S(1)}) custom-call(f32[1]{0:T(128)S(6)} %copy.12.sharp_ref, f32[1]{0:T(128)S(6)} %copy.13.off_ref, f32[1536]{0:T(1024)} %gain_i.1, f32[1536]{0:T(1024)} %gain_t.1, bf16[256,1536]{1,0:T(8,128)(2,1)} %feat_i.1, ...), custom_call_target="tpu_custom_call" | custom-call | flops 11000000512 | bytes 11000000 | tf_op jit(solution)/shard_map/siglip_grads/pallas_call | solution.py:609
  98.0 1.7 %hand_out.1 = (f32[256,1536]{1,0:T(8,128)}, f32[256,1536]{1,0:T(8,128)}, f32[48,128]{1,0:T(8,128)}, f32[48,128]{1,0:T(8,128)}) custom-call(f32[256,1536]{1,0:T(8,128)S(1)} %get-tuple-element.8.refs_0_, f32[256,1536]{1,0:T(8,128)S(1)} %get-tuple-element.9.refs_1_, f32[48,128]{1,0:T(8,128)S(1)} %get-tuple-element.10.refs_2_, ...), custom_call_target="tpu_custom_call" | custom-call | tf_op jit(solution)/shard_map/hand_out/pallas_call | solution.py:683

commit v3 on v2

--- a/solution.py
+++ b/solution.py
@@ -9,6 +9,7 @@
 from jax.sharding import PartitionSpec as P
 
 BF = jnp.bfloat16
+UNROLL = 8
 F32 = jnp.float32
 NT = (((1,), (1,)), ((), ()))
 TN = (((0,), (0,)), ((), ()))
@@ -36,8 +37,8 @@
 
 def kernel(
     scale,
-    sharp_ref,
-    off_ref,
+    sharp_hbm,
+    off_hbm,
     gain_i,
     gain_t,
     feat_i,
@@ -48,6 +49,10 @@
     gt_out,
     wi_out,
     wt_out,
+    sharp_ref,
+    off_ref,
+    gain_v,
+    small_sem,
     feats,
     weights,
     gains,
@@ -86,7 +91,8 @@
     di_rs,
     dt_ss,
     dt_rs,
-    dp_sem,
+    dp_ss,
+    dp_rs,
     w1_ss,
     w1_rs,
     w2_ss,
@@ -112,14 +118,27 @@
     rows, width = feats.shape[1], feats.shape[2]
     emb = imgs.shape[2]
 
+    small = [
+        pltpu.make_async_copy(src, dst, small_sem.at[n])
+        for n, (src, dst) in enumerate(
+            (
+                (gain_t, gain_v.at[1]),
+                (gain_i, gain_v.at[0]),
+                (sharp_hbm, sharp_ref),
+                (off_hbm, off_ref),
+            )
+        )
+    ]
+    for load in small:
+        load.start()
     loads = [
         pltpu.make_async_copy(feat_t, feats.at[1], load_sem.at[0]),
         pltpu.make_async_copy(w_t, weights.at[1], load_sem.at[1]),
         pltpu.make_async_copy(feat_i, feats.at[0], load_sem.at[2]),
         pltpu.make_async_copy(w_i, weights.at[0], load_sem.at[3]),
     ]
-    for load in loads:
-        load.start()
+    for n in (0, 2, 1, 3):
+        loads[n].start()
 
     barrier = pltpu.get_barrier_semaphore()
     partners = [device_at(x, y + d, z, c) for d in (1, 2, 3)]
@@ -131,8 +150,10 @@
         pl.semaphore_signal(
             barrier, inc=1, device_id=device, device_id_type=pl.DeviceIdType.MESH
         )
-    gains[0] = gain_i[...].reshape(1, width)
-    gains[1] = gain_t[...].reshape(1, width)
+    for load in small:
+        load.wait()
+    gains[0] = gain_v[0].reshape(1, width)
+    gains[1] = gain_v[1].reshape(1, width)
 
     step = 32
 
@@ -151,7 +172,7 @@
             act[place, r, :] = (cen * rstd * gains[t]).astype(BF)
             return 0
 
-        lax.fori_loop(0, rows // step, body, 0)
+        lax.fori_loop(0, rows // step, body, 0, unroll=UNROLL)
 
     def project(t, wait_weights, dst):
         wait_weights.wait()
@@ -172,9 +193,10 @@
             dst[r, :] = u.astype(BF)
             return 0
 
-        lax.fori_loop(0, rows // step, body, 0)
+        lax.fori_loop(0, rows // step, body, 0, unroll=UNROLL)
 
     normalize(1, loads[0])
+    normalize(0, loads[2])
     project(1, loads[1], txts.at[2 + xh])
     pl.semaphore_wait(barrier, 23)
 
@@ -211,7 +233,6 @@
         direct_text.start()
 
     t_copies[1].start()
-    normalize(0, loads[2])
     project(0, loads[3], imgs.at[0])
     half_a, half_b = pl.ds(0, rows // 2), pl.ds(rows // 2, rows // 2)
     up, down = device_at(x, y + 1, z, c), device_at(x, y + 3, z, c)
@@ -239,21 +260,25 @@
     off = off_ref[0]
     own, late = 2 + xh, 2 + ox
 
-    def pair(s, t, matching=False, fresh=False):
-        img = imgs[s]
-        sim = lax.dot_general(img, txts[t], NT, preferred_element_type=F32)
-        prob = jax.nn.sigmoid(sharp * sim + off)
-        if matching:
-            row = lax.broadcasted_iota(jnp.int32, (rows, rows), 0)
-            col = lax.broadcasted_iota(jnp.int32, (rows, rows), 1)
-            prob = prob - (row == col).astype(F32)
-        chosen = prob.astype(BF)
-        coef[s, t] = chosen
-        part = lax.dot_general(chosen, img, TN, preferred_element_type=F32)
-        if fresh:
-            d_txt[t] = part
-        else:
-            d_txt[t] += part
+    def pairs(*todo, matching=False):
+        for s, t in todo:
+            sim = lax.dot_general(imgs[s], txts[t], NT, preferred_element_type=F32)
+            prob = jax.nn.sigmoid(sharp * sim + off)
+            if matching:
+                row = lax.broadcasted_iota(jnp.int32, (rows, rows), 0)
+                col = lax.broadcasted_iota(jnp.int32, (rows, rows), 1)
+                prob = prob - (row == col).astype(F32)
+            coef[s, t] = prob.astype(BF)
+
+    def text_terms(t, shards):
+        total = lax.dot_general(
+            coef[shards[0], t], imgs[shards[0]], TN, preferred_element_type=F32
+        )
+        for s in shards[1:]:
+            total += lax.dot_general(
+                coef[s, t], imgs[s], TN, preferred_element_type=F32
+            )
+        return total
 
     def image_terms(s, dst):
         for n in range(emb // 256):
@@ -296,14 +321,12 @@
         remote(dt_send.at[2], dt_recv.at[2], dt_ss.at[2], dt_rs.at[2], partner)
     )
 
-    pair(0, own, matching=True, fresh=True)
+    pairs((0, own), matching=True)
     a_copy.wait()
     for half in (0, 1):
         for n in range(width // 256):
             cols = slice(n * 256, (n + 1) * 256)
             act_t[cols, half * rows : (half + 1) * rows] = act[half, :, cols].T
-    landed(txts.at[xh], t_recv.at[xh])
-    pair(0, xh, fresh=True)
     i_copies[0].wait_recv()
     i_copies[4].start()
     i_copies[2].wait_recv()
@@ -311,52 +334,39 @@
 
     @pl.when(c == 0)
     def _():
-        landed(txts.at[ox], t_recv.at[ox])
-        pair(0, ox, fresh=True)
-
+        landed(other_text, t_recv.at[2])
+        forward_text.start()
+
+    landed(txts.at[xh], t_recv.at[xh])
+    pairs((0, xh))
     i_copies[1].wait_recv()
     i_copies[3].wait_recv()
-    for s in (3, 1):
-        pair(s, own)
-        pair(s, xh)
-
-    @pl.when(c == 0)
-    def _():
-        pair(3, ox)
-        pair(1, ox)
-
-    landed(other_text, t_recv.at[2])
-
-    @pl.when(c == 0)
-    def _():
-        forward_text.start()
+    pairs((3, own), (1, own), (3, xh), (1, xh))
+    d_txt[xh] = text_terms(xh, (0, 1, 3))
+    landed(txts.at[ox], t_recv.at[ox])
+    pairs((0, ox), (3, ox), (1, ox))
+    d_txt[ox] = text_terms(ox, (0, 1, 3))
 
     @pl.when(c == 1)
     def _():
-        landed(txts.at[ox], t_recv.at[ox])
-        pair(0, ox, fresh=True)
-        pair(3, ox)
-        pair(1, ox)
-
-    pair(3, late, fresh=True)
+        landed(other_text, t_recv.at[2])
+
+    pairs((3, late), (1, late))
     image_terms(3, di_send.at[2])
     di_copies[0].start()
-    pair(1, late)
     image_terms(1, di_send.at[0])
     di_copies[5].start()
     i_copies[4].wait_recv()
     i_copies[5].wait_recv()
-    pair(2, xh)
-    pair(2, ox)
+    pairs((2, xh), (2, ox))
     for j in (0, 1):
-        dt_send[j] = d_txt[j].astype(BF)
+        dt_send[j] = (d_txt[j] + text_terms(j, (2,))).astype(BF)
         dt_copies[j].start()
-    pair(2, late)
-    pair(2, own)
+    pairs((2, own), (2, late), (0, late))
     image_terms(2, di_send.at[1])
     for n in (1, 6, 2, 7):
         di_copies[n].start()
-    pair(0, late)
+    d_txt[late] = text_terms(late, (0, 1, 2, 3))
 
     @pl.when(c == 0)
     def _():
@@ -377,10 +387,11 @@
             d = sharp * total(r)
             u = unit[t, r, :]
             dot = jnp.sum(u * d, axis=-1, keepdims=True)
-            dp[place, r, :] = ((d - u * dot) * inv_norm[t, r, :]).astype(BF)
+            at = pl.ds(pl.multiple_of(place * rows + i * step, step), step)
+            dp[at, :] = ((d - u * dot) * inv_norm[t, r, :]).astype(BF)
             return 0
 
-        lax.fori_loop(0, rows // step, body, 0)
+        lax.fori_loop(0, rows // step, body, 0, unroll=UNROLL)
 
     def img_total(r):
         total = d_own[r, :]
@@ -388,6 +399,7 @@
             total += di_recv[n, r, :].astype(F32)
         return total
 
+    d_txt[own] = text_terms(own, (0, 1, 2, 3))
     image_terms(0, d_own)
     for n, slot in ((0, 2), (2, 0), (1, 2), (3, 0)):
         arrived, onward = ((1, 3), (2, 4), (6, 8), (7, 9))[n]
@@ -400,11 +412,28 @@
     for n in (0, 5, 3, 8, 4, 9):
         di_copies[n].wait_recv()
     head_backward(0, img_total)
-    dp_copy = remote(dp.at[2], dp.at[1], dp_sem.at[0], dp_sem.at[1], other)
+    img_order = [lax.rem(y + d, 4) for d in (2, 1, 3, 0)]
+    txt_order = (0, 2, 1, 3)
+
+    def columns(j, core):
+        n = jnp.where(core == 0, img_order[j], txt_order[j])
+        return pl.ds(pl.multiple_of(n * 256, 256), 256)
+
+    dp_copies = [
+        remote(
+            dp.at[pl.ds(2 * rows, rows), columns(j, oc)],
+            dp.at[pl.ds(rows, rows), columns(j, oc)],
+            dp_ss.at[j],
+            dp_rs.at[j],
+            other,
+        )
+        for j in range(4)
+    ]
 
     @pl.when(c == 1)
     def _():
-        dp_copy.start()
+        for copy in dp_copies:
+            copy.start()
 
     landed(dt_recv.at[2], dt_rs.at[2])
     landed(dt_recv.at[xh], dt_rs.at[xh])
@@ -425,9 +454,9 @@
 
     @pl.when(c == 0)
     def _():
-        dp_copy.start()
-
-    landed(dp.at[1], dp_sem.at[1])
+        for copy in dp_copies:
+            copy.start()
+
 
     def along_a(d):
         return device_at(
@@ -450,12 +479,12 @@
     ]
 
     for j in range(4):
-        by_text = (0, 2, 1, 3)[j]
-        n = jnp.where(c == 0, lax.rem(y + (2, 1, 3, 0)[j], 4), by_text)
-        cols = pl.ds(pl.multiple_of(n * 256, 256), 256)
+        n = jnp.where(c == 0, img_order[j], txt_order[j])
+        cols = columns(j, c)
+        landed(dp.at[pl.ds(rows, rows), cols], dp_rs.at[j])
         part = jnp.dot(
-            act_t[:, 0:rows], dp[0, :, cols], preferred_element_type=F32
-        ) + jnp.dot(act_t[:, rows:], dp[1, :, cols], preferred_element_type=F32)
+            act_t[...], dp[0 : 2 * rows, cols], preferred_element_type=F32
+        )
         part = part.astype(BF).reshape(8, 2, 2, 48, 256)
         for xhi in range(2):
             for xlo in range(2):
@@ -466,20 +495,21 @@
 
         @pl.when(c == 0)
         def _():
-            for n in ((0, 6, 1, 7), (2, 3), (8, 9), ())[j]:
+            for n in ((0, 6, 1, 7), (2,), (8,), ())[j]:
                 w1[n].start()
 
         @pl.when(c == 1)
         def _():
-            for n in ((0, 8), (6, 2), (1, 9), (7, 3))[j]:
+            for n in ((0, 8), (6, 2), (1,), (7,))[j]:
                 w1[n].start()
 
     def features_backward(t, out):
         place = jnp.where(c == t, 0, 2)
+        dproj = dp[pl.ds(pl.multiple_of(place * rows, rows), rows), :]
         for n in range(width // 256):
             cols = slice(n * 256, (n + 1) * 256)
             d_act[:, cols] = lax.dot_general(
-                dp[place], weights[t, cols, :], NT, preferred_element_type=F32
+                dproj, weights[t, cols, :], NT, preferred_element_type=F32
             )
 
         def body(i, _):
@@ -492,7 +522,7 @@
             out[r, :] = rstd * (ghat - m1 - xhat * m2)
             return 0
 
-        lax.fori_loop(0, rows // step, body, 0)
+        lax.fori_loop(0, rows // step, body, 0, unroll=UNROLL)
 
     features_backward(0, gi_out)
     for b, arrived, onward, chunk in (
@@ -507,6 +537,9 @@
                 wb[chunk, b, zz].astype(F32) + w_pass[b, zz].astype(F32)
             ).astype(BF)
         w1[onward].start()
+        if b == 2:
+            w1[3].start()
+            w1[9].start()
     features_backward(1, gt_out)
 
     def w2_copy(b, slot, half, device):
@@ -519,6 +552,10 @@
             device,
         )
 
+    def w2_start(b, half):
+        device = device_at(jnp.where(c == 0, b, x), jnp.where(c == 0, y, b), z, c)
+        w2_copy(b, lax.rem(b + 3 - pos_b, 4), half, device).start()
+
     for b, early, late_piece in ((0, 8, 4), (2, 2, 10), (1, 9, 5), (3, 3, 11)):
         w1[early].wait_recv()
         w1[late_piece].wait_recv()
@@ -528,13 +565,8 @@
 
         @pl.when(pos_b != b)
         def _():
-            for half in (0, 1):
-                w2_copy(
-                    b,
-                    lax.rem(b + 3 - pos_b, 4),
-                    half,
-                    device_at(jnp.where(c == 0, b, x), jnp.where(c == 0, y, b), z, c),
-                ).start()
+            w2_start(b, 0)
+            w2_start(b, 1)
 
     def w3_copy(zd, cd):
         return remote(
@@ -574,7 +606,7 @@
 
     for copy in t_copies + [direct_text] + i_copies + di_copies + dt_copies:
         copy.wait_send()
-    for copy in w1 + [dp_copy]:
+    for copy in w1 + dp_copies:
         copy.wait_send()
     for half in (0, 1):
         for d in range(3):
@@ -603,7 +635,6 @@
     batch = rows * lax.axis_size("group") * lax.axis_size("blk")
     scale = math.sqrt(emb / batch)
     vmem = pl.BlockSpec(memory_space=pltpu.VMEM)
-    smem = pl.BlockSpec(memory_space=pltpu.SMEM)
     hbm = pl.BlockSpec(memory_space=pl.ANY)
     dma = pltpu.SemaphoreType.DMA
     grads = pl.pallas_call(
@@ -615,9 +646,13 @@
             pltpu.VMEM((48, 128), F32),
             pltpu.VMEM((48, 128), F32),
         ),
-        in_specs=[smem, smem, vmem, vmem, hbm, hbm, hbm, hbm],
+        in_specs=[hbm] * 8,
         out_specs=(vmem, vmem, vmem, vmem),
         scratch_shapes=[
+            pltpu.SMEM((1,), F32),
+            pltpu.SMEM((1,), F32),
+            pltpu.VMEM((2, width), F32),
+            dma((4,)),
             pltpu.VMEM((2, rows, width), BF),
             pltpu.VMEM((2, width, emb), BF),
             pltpu.VMEM((2, 1, width), F32),
@@ -637,7 +672,7 @@
             pltpu.VMEM((rows, emb), BF),
             pltpu.VMEM((3, rows, emb), BF),
             pltpu.VMEM((3, rows, emb), BF),
-            pltpu.VMEM((3, rows, emb), BF),
+            pltpu.VMEM((3 * rows, emb), BF),
             pltpu.VMEM((rows, width), F32),
             pltpu.VMEM((4, 4, 8, 2, 48, 128), BF),
             pltpu.VMEM((4, 8, 2, 48, 128), BF),
@@ -656,7 +691,8 @@
             dma((10,)),
             dma((3,)),
             dma((3,)),
-            dma((2,)),
+            dma((4,)),
+            dma((4,)),
             dma((12,)),
             dma((12,)),
             dma((3, 2)),

time: 100 us -> 95.1 us (0.951)
  the two profiles are of different devices: /device:TPU:25 before, /device:TPU:9 now
where the time goes in v3:
time: 95.1 us; the launch traced here: 95 us
  Pallas kernels  92.9 us (98%)
  between operations  2.09 us (2%)
    pallas_call x1, Pallas kernels, on_device(): pl.pallas_call(functools.partial(kernel, scale), name='siglip_grads', out...  91.2 us

profile of v3, /device:TPU:9, one launch (start us, length us, event | category | flops | bytes accessed | tf_op | source)
XLA Modules:
  0.0 95.0 jit_solution(10175351499970993401)
XLA Ops:
  1.9 91.2 %siglip_grads.1 = (f32[256,1536]{1,0:T(8,128)S(1)}, f32[256,1536]{1,0:T(8,128)S(1)}, f32[48,128]{1,0:T(8,128)S(1)}, f32[48,128]{1,0:T(8,128)S(1)}) custom-call(f32[1]{0:T(128)S(6)} %copy.12.sharp_hbm, f32[1]{0:T(128)S(6)} %copy.13.off_hbm, f32[1536]{0:T(1024)} %gain_i.1, f32[1536]{0:T(1024)} %gain_t.1, bf16[256,1536]{1,0:T(8,128)(2,1)} %feat_i.1, ...), custom_call_target="tpu_custom_call" | custom-call | flops 11000000512 | bytes 11000000 | tf_op jit(solution)/shard_map/siglip_grads/pallas_call | solution.py:640
  93.1 1.7 %hand_out.1 = (f32[256,1536]{1,0:T(8,128)}, f32[256,1536]{1,0:T(8,128)}, f32[48,128]{1,0:T(8,128)}, f32[48,128]{1,0:T(8,128)}) custom-call(f32[256,1536]{1,0:T(8,128)S(1)} %get-tuple-element.8.refs_0_, f32[256,1536]{1,0:T(8,128)S(1)} %get-tuple-element.9.refs_1_, f32[48,128]{1,0:T(8,128)S(1)} %get-tuple-element.10.refs_2_, ...), custom_call_target="tpu_custom_call" | custom-call | tf_op jit(solution)/shard_map/hand_out/pallas_call | solution.py:719

commit v4 on v3

--- a/solution.py
+++ b/solution.py
@@ -99,6 +99,7 @@
     w2_rs,
     w3_ss,
     w3_rs,
+    turn,
 ):
     k = lax.axis_index("blk")
     g = lax.axis_index("group")
@@ -232,7 +233,10 @@
     def _():
         direct_text.start()
 
-    t_copies[1].start()
+    @pl.when(c == 0)
+    def _():
+        t_copies[1].start()
+
     project(0, loads[3], imgs.at[0])
     half_a, half_b = pl.ds(0, rows // 2), pl.ds(rows // 2, rows // 2)
     up, down = device_at(x, y + 1, z, c), device_at(x, y + 3, z, c)
@@ -306,17 +310,17 @@
             )
         )
     ]
-    dt_copies = []
-    for j in (0, 1):
-        dt_copies.append(
-            remote(
-                dt_send.at[j],
-                dt_recv.at[jnp.where(c == 0, xh, j)],
-                dt_ss.at[j],
-                dt_rs.at[jnp.where(c == 0, xh, j)],
-                {"blk": behind, "group": y * 2 + jnp.where(c == 0, j, xh)},
-            )
-        )
+    def prev_copy(j):
+        slot = jnp.where(c == 0, xh, j)
+        owner = {"blk": behind, "group": y * 2 + jnp.where(c == 0, j, xh)}
+        return remote(
+            dt_send.at[j], dt_recv.at[slot], dt_ss.at[j], dt_rs.at[slot], owner
+        )
+
+    def start_prev(j):
+        prev_copy(j).start()
+
+    dt_copies = [prev_copy(0), prev_copy(1)]
     dt_copies.append(
         remote(dt_send.at[2], dt_recv.at[2], dt_ss.at[2], dt_rs.at[2], partner)
     )
@@ -332,6 +336,10 @@
     i_copies[2].wait_recv()
     i_copies[5].start()
 
+    @pl.when(c == 1)
+    def _():
+        t_copies[1].start()
+
     @pl.when(c == 0)
     def _():
         landed(other_text, t_recv.at[2])
@@ -358,10 +366,12 @@
     di_copies[5].start()
     i_copies[4].wait_recv()
     i_copies[5].wait_recv()
-    pairs((2, xh), (2, ox))
-    for j in (0, 1):
-        dt_send[j] = (d_txt[j] + text_terms(j, (2,))).astype(BF)
-        dt_copies[j].start()
+    pairs((2, ox))
+    dt_send[ox] = (d_txt[ox] + text_terms(ox, (2,))).astype(BF)
+    start_prev(ox)
+    pairs((2, xh))
+    dt_send[xh] = (d_txt[xh] + text_terms(xh, (2,))).astype(BF)
+    start_prev(xh)
     pairs((2, own), (2, late), (0, late))
     image_terms(2, di_send.at[1])
     for n in (1, 6, 2, 7):
@@ -563,10 +573,20 @@
             total = wb[pos_a, b, zz].astype(F32) + wr1[0, b, zz].astype(F32)
             s1[b, zz] = (total + wr1[1, b, zz].astype(F32)).astype(BF)
 
-        @pl.when(pos_b != b)
-        def _():
-            w2_start(b, 0)
-            w2_start(b, 1)
+        if b == 2:
+            for copy in w1:
+                copy.wait_send()
+            pl.semaphore_signal(
+                turn, inc=1, device_id=other, device_id_type=pl.DeviceIdType.MESH
+            )
+
+    pl.semaphore_wait(turn, 1)
+    for half in (0, 1):
+        for b in (0, 2, 1, 3):
+
+            @pl.when(pos_b != b)
+            def _():
+                w2_start(b, half)
 
     def w3_copy(zd, cd):
         return remote(
@@ -606,7 +626,7 @@
 
     for copy in t_copies + [direct_text] + i_copies + di_copies + dt_copies:
         copy.wait_send()
-    for copy in w1 + dp_copies:
+    for copy in dp_copies:
         copy.wait_send()
     for half in (0, 1):
         for d in range(3):
@@ -699,6 +719,7 @@
             dma((3, 2)),
             dma((8, 2)),
             dma((2, 8)),
+            pltpu.SemaphoreType.REGULAR,
         ],
         compiler_params=pltpu.CompilerParams(
             collective_id=0, has_side_effects=True, vmem_limit_bytes=54 << 20

time: 95.1 us -> 91.7 us (0.964)
  the two profiles are of different devices: /device:TPU:9 before, /device:TPU:1 now
where the time goes in v4:
time: 91.7 us; the launch traced here: 91.6 us
  Pallas kernels  89.5 us (98%)
  between operations  2.09 us (2%)
    pallas_call x1, Pallas kernels, on_device(): pl.pallas_call(functools.partial(kernel, scale), name='siglip_grads', out...  87.8 us

profile of v4, /device:TPU:1, one launch (start us, length us, event | category | flops | bytes accessed | tf_op | source)
XLA Modules:
  0.0 91.6 jit_solution(4889657319322339328)
XLA Ops:
  1.9 87.8 %siglip_grads.1 = (f32[256,1536]{1,0:T(8,128)S(1)}, f32[256,1536]{1,0:T(8,128)S(1)}, f32[48,128]{1,0:T(8,128)S(1)}, f32[48,128]{1,0:T(8,128)S(1)}) custom-call(f32[1]{0:T(128)S(6)} %copy.12.sharp_hbm, f32[1]{0:T(128)S(6)} %copy.13.off_hbm, f32[1536]{0:T(1024)} %gain_i.1, f32[1536]{0:T(1024)} %gain_t.1, bf16[256,1536]{1,0:T(8,128)(2,1)} %feat_i.1, ...), custom_call_target="tpu_custom_call" | custom-call | flops 11000000512 | bytes 11000000 | tf_op jit(solution)/shard_map/siglip_grads/pallas_call | solution.py:660
  89.7 1.7 %hand_out.1 = (f32[256,1536]{1,0:T(8,128)}, f32[256,1536]{1,0:T(8,128)}, f32[48,128]{1,0:T(8,128)}, f32[48,128]{1,0:T(8,128)}) custom-call(f32[256,1536]{1,0:T(8,128)S(1)} %get-tuple-element.8.refs_0_, f32[256,1536]{1,0:T(8,128)S(1)} %get-tuple-element.9.refs_1_, f32[48,128]{1,0:T(8,128)S(1)} %get-tuple-element.10.refs_2_, ...), custom_call_target="tpu_custom_call" | custom-call | tf_op jit(solution)/shard_map/hand_out/pallas_call | solution.py:740

commit v5 on v4

--- a/solution.py
+++ b/solution.py
@@ -81,6 +81,20 @@
     wr2,
     s2,
     wr3,
+    wz,
+    rz,
+    sa,
+    ra,
+    sb,
+    rb,
+    top,
+    wz_ss,
+    wz_rs,
+    ra_ss,
+    ra_rs,
+    rb_ss,
+    rb_rs,
+    top_sem,
     load_sem,
     i_send,
     i_recv,
@@ -495,13 +509,14 @@
         part = jnp.dot(
             act_t[...], dp[0 : 2 * rows, cols], preferred_element_type=F32
         )
-        part = part.astype(BF).reshape(8, 2, 2, 48, 256)
+        part = part.astype(BF).reshape(8, 2, 96, 256)
         for xhi in range(2):
             for xlo in range(2):
                 px = 2 * xhi + xlo
-                wb[jnp.where(c == 0, n, px), jnp.where(c == 0, px, n)] = part[
-                    :, xlo, :, :, xhi * 128 : (xhi + 1) * 128
-                ]
+                at_a, at_b = jnp.where(c == 0, n, px), jnp.where(c == 0, px, n)
+                block = part[:, xlo, :, xhi * 128 : (xhi + 1) * 128]
+                wb[at_a, at_b] = block[:, 16:]
+                wz[:, at_a, at_b] = block[:, :16]
 
         @pl.when(c == 0)
         def _():
@@ -534,6 +549,19 @@
 
         lax.fori_loop(0, rows // step, body, 0, unroll=UNROLL)
 
+    wz_copies = []
+    for d in (4, 3, 5, 2, 6, 1, 7):
+        wz_copies.append(
+            remote(
+                wz.at[lax.rem(z + d, 8)],
+                rz.at[z],
+                wz_ss.at[d - 1],
+                wz_rs.at[z],
+                device_at(x, y, z + d, c),
+            )
+        )
+        wz_copies[-1].start()
+    rz[z] = wz[z]
     features_backward(0, gi_out)
     for b, arrived, onward, chunk in (
         (0, 0, 4, fore),
@@ -588,10 +616,36 @@
             def _():
                 w2_start(b, half)
 
+    for d in range(1, 8):
+        src = lax.rem(z + d, 8)
+        landed(rz.at[src], wz_rs.at[src])
+    for a in range(4):
+        for b in range(4):
+            total = rz[0, a, b].astype(F32)
+            for zs in range(1, 8):
+                total += rz[zs, a, b].astype(F32)
+            sa[a, b] = total.astype(BF)
+    small_copies = [
+        remote(
+            sa.at[lax.rem(pos_a + d, 4)],
+            ra.at[d - 1],
+            ra_ss.at[d - 1],
+            ra_rs.at[d - 1],
+            along_a(d),
+        )
+        for d in (2, 1, 3)
+    ]
+    for copy in small_copies:
+        copy.start()
+
     def w3_copy(zd, cd):
+        if cd == 0:
+            src, dst = s2.at[zd, pl.ds(0, 32)], wr3.at[c, z, pl.ds(16, 32)]
+        else:
+            src, dst = s2.at[zd, pl.ds(32, 48)], wr3.at[c, z]
         return remote(
-            s2.at[zd, cd],
-            wr3.at[c, z],
+            src,
+            dst,
             w3_ss.at[zd, cd],
             w3_rs.at[c, z],
             {"blk": zd * 4 + xl * 2 + cd, "group": g},
@@ -611,22 +665,77 @@
                 def _():
                     w3_copy(zd, cd).start()
 
-    wr3[c, z] = s2[z, c]
-    for t, out in ((0, wi_out), (1, wt_out)):
-        for zs in range(8):
-
-            @pl.when((zs != z) | (t != c))
-            def _():
-                landed(wr3.at[t, zs], w3_rs.at[t, zs])
-
-        total = wr3[t, 0].astype(F32)
-        for zs in range(1, 8):
-            total += wr3[t, zs].astype(F32)
-        out[...] = total * scale
+    @pl.when(c == 0)
+    def _():
+        wr3[0, z, 16:48] = s2[z, 0:32]
+
+    @pl.when(c == 1)
+    def _():
+        wr3[1, z] = s2[z, 32:80]
+
+    for d in (1, 2, 3):
+        landed(ra.at[d - 1], ra_rs.at[d - 1])
+    for b in range(4):
+        total = sa[pos_a, b].astype(F32)
+        for d in range(3):
+            total += ra[d, b].astype(F32)
+        sb[b] = total.astype(BF)
+    for d in (2, 1, 3):
+        small_copies.append(
+            remote(
+                sb.at[lax.rem(pos_b + d, 4)],
+                rb.at[d - 1],
+                rb_ss.at[d - 1],
+                rb_rs.at[d - 1],
+                device_at(
+                    jnp.where(c == 0, x + d, x), jnp.where(c == 0, y, y + d), z, c
+                ),
+            )
+        )
+        small_copies[-1].start()
+    for d in (1, 2, 3):
+        landed(rb.at[d - 1], rb_rs.at[d - 1])
+    total = sb[pos_b].astype(F32)
+    for d in range(3):
+        total += rb[d].astype(F32)
+    top[c] = total
+    top_copy = remote(top.at[1], top.at[1], top_sem.at[0], top_sem.at[1], other)
+
+    @pl.when(c == 1)
+    def _():
+        top_copy.start()
+        for t, out in ((0, wi_out), (1, wt_out)):
+            for zs in range(8):
+
+                @pl.when((zs != z) | (t == 0))
+                def _():
+                    landed(wr3.at[t, zs], w3_rs.at[t, zs])
+
+            total = wr3[t, 0].astype(F32)
+            for zs in range(1, 8):
+                total += wr3[t, zs].astype(F32)
+            out[...] = total * scale
+        top_copy.wait_send()
+
+    @pl.when(c == 0)
+    def _():
+        top_copy.wait_recv()
+        for t, out in ((0, wi_out), (1, wt_out)):
+            for zs in range(8):
+
+                @pl.when((zs != z) | (t == 1))
+                def _():
+                    landed(wr3.at[t, zs, pl.ds(16, 32)], w3_rs.at[t, zs])
+
+            total = wr3[t, 0, 16:48].astype(F32)
+            for zs in range(1, 8):
+                total += wr3[t, zs, 16:48].astype(F32)
+            out[16:48] = total * scale
+            out[0:16] = top[t] * scale
 
     for copy in t_copies + [direct_text] + i_copies + di_copies + dt_copies:
         copy.wait_send()
-    for copy in dp_copies:
+    for copy in dp_copies + wz_copies + small_copies:
         copy.wait_send()
     for half in (0, 1):
         for d in range(3):
@@ -694,13 +803,27 @@
             pltpu.VMEM((3, rows, emb), BF),
             pltpu.VMEM((3 * rows, emb), BF),
             pltpu.VMEM((rows, width), F32),
-            pltpu.VMEM((4, 4, 8, 2, 48, 128), BF),
-            pltpu.VMEM((4, 8, 2, 48, 128), BF),
-            pltpu.VMEM((2, 4, 8, 2, 48, 128), BF),
-            pltpu.VMEM((4, 8, 2, 48, 128), BF),
-            pltpu.VMEM((3, 8, 2, 48, 128), BF),
-            pltpu.VMEM((8, 2, 48, 128), BF),
+            pltpu.VMEM((4, 4, 8, 80, 128), BF),
+            pltpu.VMEM((4, 8, 80, 128), BF),
+            pltpu.VMEM((2, 4, 8, 80, 128), BF),
+            pltpu.VMEM((4, 8, 80, 128), BF),
+            pltpu.VMEM((3, 8, 80, 128), BF),
+            pltpu.VMEM((8, 80, 128), BF),
             pltpu.VMEM((2, 8, 48, 128), BF),
+            pltpu.VMEM((8, 4, 4, 16, 128), BF),
+            pltpu.VMEM((8, 4, 4, 16, 128), BF),
+            pltpu.VMEM((4, 4, 16, 128), BF),
+            pltpu.VMEM((3, 4, 16, 128), BF),
+            pltpu.VMEM((4, 16, 128), BF),
+            pltpu.VMEM((3, 16, 128), BF),
+            pltpu.VMEM((2, 16, 128), F32),
+            dma((7,)),
+            dma((8,)),
+            dma((3,)),
+            dma((3,)),
+            dma((3,)),
+            dma((3,)),
+            dma((2,)),
             dma((4,)),
             dma((6,)),
             dma((6,)),

time: 91.7 us -> 89.6 us (0.977)
  Pallas kernels: 89.5 us -> 87.4 us
    pallas_call x1, Pallas kernels: 87.8 us -> 85.7 us  [on_device(): pl.pallas_call(functools.partial(kernel, scale), name='siglip_grads', out...]
where the time goes in v5:
time: 89.6 us; the launch traced here: 89.5 us
  Pallas kernels  87.4 us (98%)
  between operations  2.09 us (2%)
    pallas_call x1, Pallas kernels, on_device(): pl.pallas_call(functools.partial(kernel, scale), name='siglip_grads', out...  85.7 us

profile of v5, /device:TPU:1, one launch (start us, length us, event | category | flops | bytes accessed | tf_op | source)
XLA Modules:
  0.0 89.5 jit_solution(17727118487556658262)
XLA Ops:
  1.9 85.7 %siglip_grads.1 = (f32[256,1536]{1,0:T(8,128)S(1)}, f32[256,1536]{1,0:T(8,128)S(1)}, f32[48,128]{1,0:T(8,128)S(1)}, f32[48,128]{1,0:T(8,128)S(1)}) custom-call(f32[1]{0:T(128)S(6)} %copy.12.sharp_hbm, f32[1]{0:T(128)S(6)} %copy.13.off_hbm, f32[1536]{0:T(1024)} %gain_i.1, f32[1536]{0:T(1024)} %gain_t.1, bf16[256,1536]{1,0:T(8,128)(2,1)} %feat_i.1, ...), custom_call_target="tpu_custom_call" | custom-call | flops 11000000512 | bytes 11000000 | tf_op jit(solution)/shard_map/siglip_grads/pallas_call | solution.py:769
  87.6 1.7 %hand_out.1 = (f32[256,1536]{1,0:T(8,128)}, f32[256,1536]{1,0:T(8,128)}, f32[48,128]{1,0:T(8,128)}, f32[48,128]{1,0:T(8,128)}) custom-call(f32[256,1536]{1,0:T(8,128)S(1)} %get-tuple-element.8.refs_0_, f32[256,1536]{1,0:T(8,128)S(1)} %get-tuple-element.9.refs_1_, f32[48,128]{1,0:T(8,128)S(1)} %get-tuple-element.10.refs_2_, ...), custom_call_target="tpu_custom_call" | custom-call | tf_op jit(solution)/shard_map/hand_out/pallas_call | solution.py:863

commit v6 on v5

--- a/solution.py
+++ b/solution.py
@@ -152,7 +152,7 @@
         pltpu.make_async_copy(feat_i, feats.at[0], load_sem.at[2]),
         pltpu.make_async_copy(w_i, weights.at[0], load_sem.at[3]),
     ]
-    for n in (0, 2, 1, 3):
+    for n in (0, 2, 1):
         loads[n].start()
 
     barrier = pltpu.get_barrier_semaphore()
@@ -191,6 +191,8 @@
 
     def project(t, wait_weights, dst):
         wait_weights.wait()
+        if t == 1:
+            loads[3].start()
         place = jnp.where(c == t, 0, 2)
         for n in range(emb // 256):
             cols = slice(n * 256, (n + 1) * 256)
@@ -212,40 +214,41 @@
 
     normalize(1, loads[0])
     normalize(0, loads[2])
-    project(1, loads[1], txts.at[2 + xh])
+    project(1, loads[1], txts.at[0])
     pl.semaphore_wait(barrier, 23)
 
-    own_text = txts.at[2 + xh]
-    other_text = txts.at[2 + ox]
+    own_text = txts.at[0]
+    other_text = txts.at[1]
     t_copies = [
         remote(
             own_text,
-            txts.at[xh],
+            txts.at[2],
             t_send.at[0],
-            t_recv.at[xh],
+            t_recv.at[0],
             {"blk": ahead, "group": g},
         ),
-        remote(own_text, txts.at[2 + xh], t_send.at[1], t_recv.at[2], partner),
+        remote(own_text, other_text, t_send.at[1], t_recv.at[2], partner),
     ]
-    t_copies[0].start()
     direct_text = remote(
         own_text,
-        txts.at[xh],
+        txts.at[3],
         t_send.at[2],
-        t_recv.at[xh],
+        t_recv.at[1],
         {"blk": ahead, "group": y * 2 + ox},
     )
     forward_text = remote(
         other_text,
-        txts.at[ox],
+        txts.at[3],
         t_send.at[2],
-        t_recv.at[ox],
+        t_recv.at[1],
         {"blk": ahead, "group": g},
     )
 
     @pl.when(c == 1)
     def _():
         direct_text.start()
+
+    t_copies[0].start()
 
     @pl.when(c == 0)
     def _():
@@ -276,7 +279,7 @@
 
     sharp = sharp_ref[0]
     off = off_ref[0]
-    own, late = 2 + xh, 2 + ox
+    own, late, prev, cross = 0, 1, 2, 3
 
     def pairs(*todo, matching=False):
         for s, t in todo:
@@ -324,17 +327,18 @@
             )
         )
     ]
-    def prev_copy(j):
-        slot = jnp.where(c == 0, xh, j)
-        owner = {"blk": behind, "group": y * 2 + jnp.where(c == 0, j, xh)}
-        return remote(
-            dt_send.at[j], dt_recv.at[slot], dt_ss.at[j], dt_rs.at[slot], owner
-        )
-
-    def start_prev(j):
-        prev_copy(j).start()
-
-    dt_copies = [prev_copy(0), prev_copy(1)]
+    dt_copies = []
+    for j in (0, 1):
+        owner = y * 2 + (xh if j == 0 else jnp.where(c == 0, ox, xh))
+        dt_copies.append(
+            remote(
+                dt_send.at[j],
+                dt_recv.at[j],
+                dt_ss.at[j],
+                dt_rs.at[j],
+                {"blk": behind, "group": owner},
+            )
+        )
     dt_copies.append(
         remote(dt_send.at[2], dt_recv.at[2], dt_ss.at[2], dt_rs.at[2], partner)
     )
@@ -359,15 +363,15 @@
         landed(other_text, t_recv.at[2])
         forward_text.start()
 
-    landed(txts.at[xh], t_recv.at[xh])
-    pairs((0, xh))
+    landed(txts.at[2], t_recv.at[0])
+    pairs((0, prev))
     i_copies[1].wait_recv()
     i_copies[3].wait_recv()
-    pairs((3, own), (1, own), (3, xh), (1, xh))
-    d_txt[xh] = text_terms(xh, (0, 1, 3))
-    landed(txts.at[ox], t_recv.at[ox])
-    pairs((0, ox), (3, ox), (1, ox))
-    d_txt[ox] = text_terms(ox, (0, 1, 3))
+    pairs((3, own), (1, own), (3, prev), (1, prev))
+    d_txt[prev] = text_terms(prev, (0, 1, 3))
+    landed(txts.at[3], t_recv.at[1])
+    pairs((0, cross), (3, cross), (1, cross))
+    d_txt[cross] = text_terms(cross, (0, 1, 3))
 
     @pl.when(c == 1)
     def _():
@@ -380,12 +384,11 @@
     di_copies[5].start()
     i_copies[4].wait_recv()
     i_copies[5].wait_recv()
-    pairs((2, ox))
-    dt_send[ox] = (d_txt[ox] + text_terms(ox, (2,))).astype(BF)
-    start_prev(ox)
-    pairs((2, xh))
-    dt_send[xh] = (d_txt[xh] + text_terms(xh, (2,))).astype(BF)
-    start_prev(xh)
+    pairs((2, cross), (2, prev))
+    dt_send[1] = (d_txt[cross] + text_terms(cross, (2,))).astype(BF)
+    dt_copies[1].start()
+    dt_send[0] = (d_txt[prev] + text_terms(prev, (2,))).astype(BF)
+    dt_copies[0].start()
     pairs((2, own), (2, late), (0, late))
     image_terms(2, di_send.at[1])
     for n in (1, 6, 2, 7):
@@ -394,13 +397,13 @@
 
     @pl.when(c == 0)
     def _():
-        landed(dt_recv.at[ox], dt_rs.at[ox])
-        dt_send[2] = (d_txt[2 + ox] + dt_recv[ox].astype(F32)).astype(BF)
+        landed(dt_recv.at[1], dt_rs.at[1])
+        dt_send[2] = (d_txt[late] + dt_recv[1].astype(F32)).astype(BF)
         dt_copies[2].start()
 
     @pl.when(c == 1)
     def _():
-        dt_send[2] = d_txt[2 + ox].astype(BF)
+        dt_send[2] = d_txt[late].astype(BF)
         dt_copies[2].start()
 
     def head_backward(t, total):
@@ -460,18 +463,17 @@
             copy.start()
 
     landed(dt_recv.at[2], dt_rs.at[2])
-    landed(dt_recv.at[xh], dt_rs.at[xh])
+    landed(dt_recv.at[0], dt_rs.at[0])
 
     @pl.when(c == 1)
     def _():
-        landed(dt_recv.at[ox], dt_rs.at[ox])
-
-    first = jnp.where(c == 0, xh, 0)
+        landed(dt_recv.at[1], dt_rs.at[1])
+
     both = c.astype(F32)
 
     def txt_total(r):
-        total = d_txt[2 + xh, r, :] + dt_recv[2, r, :].astype(F32)
-        total += dt_recv[first, r, :].astype(F32)
+        total = d_txt[own, r, :] + dt_recv[2, r, :].astype(F32)
+        total += dt_recv[0, r, :].astype(F32)
         return total + both * dt_recv[1, r, :].astype(F32)
 
     head_backward(1, txt_total)
@@ -749,9 +751,17 @@
 
 
 def hand_out(*refs):
-    copies = [
-        pltpu.make_async_copy(refs[n], refs[4 + n], refs[8].at[n]) for n in range(4)
-    ]
+    copies = []
+    for n in range(4):
+        parts = 4 if n < 2 else 1
+        size = refs[n].shape[0] // parts
+        for i in range(parts):
+            part = pl.ds(i * size, size)
+            copies.append(
+                pltpu.make_async_copy(
+                    refs[n].at[part], refs[4 + n].at[part], refs[8].at[n, i]
+                )
+            )
     for copy in copies:
         copy.start()
     for copy in copies:
@@ -866,7 +876,7 @@
         out_shape=tuple(jax.ShapeDtypeStruct(a.shape, a.dtype) for a in grads),
         in_specs=[hbm] * 4,
         out_specs=(hbm,) * 4,
-        scratch_shapes=[dma((4,))],
+        scratch_shapes=[dma((4, 4))],
         compiler_params=pltpu.CompilerParams(vmem_limit_bytes=1 << 20),
     )(*grads)
 

time: 89.6 us -> 87.2 us (0.973)
  Pallas kernels: 87.4 us -> 85 us
    pallas_call x1, Pallas kernels: 85.7 us -> 83.2 us  [on_device(): pl.pallas_call(functools.partial(kernel, scale), name='siglip_grads', out...]
where the time goes in v6:
time: 87.2 us; the launch traced here: 87.1 us
  Pallas kernels  85 us (97%)
  between operations  2.09 us (2%)
    pallas_call x1, Pallas kernels, on_device(): pl.pallas_call(functools.partial(kernel, scale), name='siglip_grads', out...  83.2 us
    pallas_call x1, Pallas kernels, on_device(): pl.pallas_call(hand_out, name='hand_out', out_shape=tuple((jax.ShapeDtype...  1.8 us

profile of v6, /device:TPU:1, one launch (start us, length us, event | category | flops | bytes accessed | tf_op | source)
XLA Modules:
  0.0 87.1 jit_solution(2782601895718258868)
XLA Ops:
  1.9 83.2 %siglip_grads.1 = (f32[256,1536]{1,0:T(8,128)S(1)}, f32[256,1536]{1,0:T(8,128)S(1)}, f32[48,128]{1,0:T(8,128)S(1)}, f32[48,128]{1,0:T(8,128)S(1)}) custom-call(f32[1]{0:T(128)S(6)} %copy.12.sharp_hbm, f32[1]{0:T(128)S(6)} %copy.13.off_hbm, f32[1536]{0:T(1024)} %gain_i.1, f32[1536]{0:T(1024)} %gain_t.1, bf16[256,1536]{1,0:T(8,128)(2,1)} %feat_i.1, ...), custom_call_target="tpu_custom_call" | custom-call | flops 11000000512 | bytes 11000000 | tf_op jit(solution)/shard_map/siglip_grads/pallas_call | solution.py:779
  85.1 1.8 %hand_out.1 = (f32[256,1536]{1,0:T(8,128)}, f32[256,1536]{1,0:T(8,128)}, f32[48,128]{1,0:T(8,128)}, f32[48,128]{1,0:T(8,128)}) custom-call(f32[256,1536]{1,0:T(8,128)S(1)} %get-tuple-element.8.refs_0_, f32[256,1536]{1,0:T(8,128)S(1)} %get-tuple-element.9.refs_1_, f32[48,128]{1,0:T(8,128)S(1)} %get-tuple-element.10.refs_2_, ...), custom_call_target="tpu_custom_call" | custom-call | tf_op jit(solution)/shard_map/hand_out/pallas_call | solution.py:873

commit v7 on v6

--- a/solution.py
+++ b/solution.py
@@ -462,28 +462,6 @@
         for copy in dp_copies:
             copy.start()
 
-    landed(dt_recv.at[2], dt_rs.at[2])
-    landed(dt_recv.at[0], dt_rs.at[0])
-
-    @pl.when(c == 1)
-    def _():
-        landed(dt_recv.at[1], dt_rs.at[1])
-
-    both = c.astype(F32)
-
-    def txt_total(r):
-        total = d_txt[own, r, :] + dt_recv[2, r, :].astype(F32)
-        total += dt_recv[0, r, :].astype(F32)
-        return total + both * dt_recv[1, r, :].astype(F32)
-
-    head_backward(1, txt_total)
-
-    @pl.when(c == 0)
-    def _():
-        for copy in dp_copies:
-            copy.start()
-
-
     def along_a(d):
         return device_at(
             jnp.where(c == 0, x, x + d), jnp.where(c == 0, y + d, y), z, c
@@ -504,7 +482,7 @@
         for n, (src, dst, device) in enumerate(pieces)
     ]
 
-    for j in range(4):
+    def weight_terms(j):
         n = jnp.where(c == 0, img_order[j], txt_order[j])
         cols = columns(j, c)
         landed(dp.at[pl.ds(rows, rows), cols], dp_rs.at[j])
@@ -550,6 +528,39 @@
             return 0
 
         lax.fori_loop(0, rows // step, body, 0, unroll=UNROLL)
+
+    @pl.when(c == 0)
+    def _():
+        weight_terms(0)
+
+    landed(dt_recv.at[2], dt_rs.at[2])
+    landed(dt_recv.at[0], dt_rs.at[0])
+
+    @pl.when(c == 1)
+    def _():
+        landed(dt_recv.at[1], dt_rs.at[1])
+
+    both = c.astype(F32)
+
+    def txt_total(r):
+        total = d_txt[own, r, :] + dt_recv[2, r, :].astype(F32)
+        total += dt_recv[0, r, :].astype(F32)
+        return total + both * dt_recv[1, r, :].astype(F32)
+
+    head_backward(1, txt_total)
+
+    @pl.when(c == 0)
+    def _():
+        for copy in dp_copies:
+            copy.start()
+
+
+    @pl.when(c == 1)
+    def _():
+        weight_terms(0)
+
+    for j in (1, 2, 3):
+        weight_terms(j)
 
     wz_copies = []
     for d in (4, 3, 5, 2, 6, 1, 7):

time: 87.2 us -> 86.3 us (0.990)
  Pallas kernels: 85 us -> 84.1 us
    pallas_call x1, Pallas kernels: 83.2 us -> 82.3 us  [on_device(): pl.pallas_call(functools.partial(kernel, scale), name='siglip_grads', out...]
where the time goes in v7:
time: 86.3 us; the launch traced here: 86.2 us
  Pallas kernels  84.1 us (97%)
  between operations  2.09 us (2%)
    pallas_call x1, Pallas kernels, on_device(): pl.pallas_call(functools.partial(kernel, scale), name='siglip_grads', out...  82.3 us
    pallas_call x1, Pallas kernels, on_device(): pl.pallas_call(hand_out, name='hand_out', out_shape=tuple((jax.ShapeDtype...  1.8 us

profile of v7, /device:TPU:1, one launch (start us, length us, event | category | flops | bytes accessed | tf_op | source)
XLA Modules:
  0.0 86.2 jit_solution(8003204088210415517)
XLA Ops:
  1.9 82.3 %siglip_grads.1 = (f32[256,1536]{1,0:T(8,128)S(1)}, f32[256,1536]{1,0:T(8,128)S(1)}, f32[48,128]{1,0:T(8,128)S(1)}, f32[48,128]{1,0:T(8,128)S(1)}) custom-call(f32[1]{0:T(128)S(6)} %copy.12.sharp_hbm, f32[1]{0:T(128)S(6)} %copy.13.off_hbm, f32[1536]{0:T(1024)} %gain_i.1, f32[1536]{0:T(1024)} %gain_t.1, bf16[256,1536]{1,0:T(8,128)(2,1)} %feat_i.1, ...), custom_call_target="tpu_custom_call" | custom-call | flops 11000000512 | bytes 11000000 | tf_op jit(solution)/shard_map/siglip_grads/pallas_call | solution.py:790
  84.2 1.8 %hand_out.1 = (f32[256,1536]{1,0:T(8,128)}, f32[256,1536]{1,0:T(8,128)}, f32[48,128]{1,0:T(8,128)}, f32[48,128]{1,0:T(8,128)}) custom-call(f32[256,1536]{1,0:T(8,128)S(1)} %get-tuple-element.8.refs_0_, f32[256,1536]{1,0:T(8,128)S(1)} %get-tuple-element.9.refs_1_, f32[48,128]{1,0:T(8,128)S(1)} %get-tuple-element.10.refs_2_, ...), custom_call_target="tpu_custom_call" | custom-call | tf_op jit(solution)/shard_map/hand_out/pallas_call | solution.py:884
